TPU v7x, 128 devices: a whole 4x4x4 slice. The times are simulated.
128 devices in a mesh: seq: 32 (over y, x, core), dp: 4 (over z).
Axes of the slice: x: 4, y: 4, z: 4, core: 2. Of those that a mesh axis runs over, the one named last changes fastest.
Arguments:
- query: bfloat16 [4, 4096, 2048], P('dp', 'seq'), may hold values from -90 to 90
- keys: bfloat16 [4, 4096, 512], P('dp', 'seq'), may hold values from -5 to 5
- values: bfloat16 [4, 4096, 512], P('dp', 'seq'), may hold values from -6 to 6
- output_gradient: bfloat16 [4, 4096, 2048], P('dp', 'seq'), may hold values from -6 to 6
- forward_output: bfloat16 [4, 4096, 2048], P('dp', 'seq'), may hold values from -6 to 6
- doc_ids: int32 [4, 4096], P('dp', 'seq'), may hold values from 0 to 7, never falling along the last dimension, each value on 1 to 2048 neighbouring positions
Outputs:
- grad_query: bfloat16 [4, 4096, 2048], P('dp', 'seq')
- grad_keys: bfloat16 [4, 4096, 512], P('dp', 'seq')
- grad_values: bfloat16 [4, 4096, 512], P('dp', 'seq')
Inputs may be any that keep to these rules, and one draw needn't show every extreme that they name: `doc_ids`: document numbers never fall along a sequence; each document has 1 to 2048 tokens, and one document of each sequence has exactly 2048.
All inputs are finite; a program needn't handle non-finite values.
Results may differ from a plain program's by a relative error of at most 0.0049.
Values may be sent and summed in bfloat16 or wider, within the bound.
A program may use at most 128 MiB of HBM per device.

v0:
```python
import math

import jax
import jax.numpy as jnp
from jax import lax
from jax.sharding import PartitionSpec as P

HEAD_WIDTH = 128


MASKED_LOW = -1e30


def attend_grads(
    q_heads, dout_heads, out_heads, key_rows, value_rows, query_ids, key_ids, first_row
):
    tok_rows = q_heads.shape[0]
    kv_heads = q_heads.shape[1]
    token_length = key_rows.shape[0]
    softmax_scale = 1.0 / math.sqrt(HEAD_WIDTH)
    block_len = min(512, token_length)
    blocks = token_length // block_len
    query_pos = first_row + jnp.arange(tok_rows, dtype=jnp.int32)
    row_dots = jnp.sum(dout_heads.astype(jnp.float32) * out_heads.astype(jnp.float32), axis=3)
    row_dots = jnp.transpose(row_dots, (1, 2, 0))
    key_blocks = key_rows.reshape(blocks, block_len, kv_heads, HEAD_WIDTH)
    value_blocks = value_rows.reshape(blocks, block_len, kv_heads, HEAD_WIDTH)
    id_blocks = key_ids.reshape(blocks, block_len)
    pos_blocks = jnp.arange(token_length, dtype=jnp.int32).reshape(blocks, block_len)

    def permitted(id_block, pos_block):
        return (id_block[None, :] == query_ids[:, None]) & (
            pos_block[None, :] <= query_pos[:, None]
        )

    def scores(key_block, allowed):
        logits = (
            jnp.einsum("tkgd,skd->kgts", q_heads, key_block, preferred_element_type=jnp.float32)
            * softmax_scale
        )
        return (logits, allowed[None, None])

    def stats_step(state_pair, block_args):
        allowed_now = permitted(block_args[1], block_args[2])

        def update(pair):
            run_max, run_sum = pair
            logits, allowed = scores(block_args[0], allowed_now)
            logits = jnp.where(allowed, logits, MASKED_LOW)
            new_max = jnp.maximum(run_max, jnp.max(logits, axis=3))
            shifted = jnp.where(allowed, jnp.exp(logits - new_max[..., None]), 0.0)
            return (new_max, run_sum * jnp.exp(run_max - new_max) + jnp.sum(shifted, axis=3))

        def keep(pair):
            return pair

        return (lax.cond(jnp.any(allowed_now), update, keep, state_pair), None)

    stat_shape = (kv_heads, q_heads.shape[2], tok_rows)
    start_state = (
        jnp.full(stat_shape, MASKED_LOW, jnp.float32),
        jnp.zeros(stat_shape, jnp.float32),
    )
    (run_max, run_sum), unused = lax.scan(
        stats_step, start_state, (key_blocks, id_blocks, pos_blocks)
    )
    log_total = run_max + jnp.log(run_sum)

    def grad_step(dq_acc, block_args):
        key_block, value_block, id_block, pos_block = block_args
        allowed_now = permitted(id_block, pos_block)

        def work(dq_now):
            logits, allowed = scores(key_block, allowed_now)
            attn_probs = jnp.where(allowed, jnp.exp(logits - log_total[..., None]), 0.0)
            probs_low = attn_probs.astype(jnp.bfloat16)
            dv_block = jnp.einsum(
                "kgts,tkgd->skd", probs_low, dout_heads, preferred_element_type=jnp.float32
            )
            prob_grads = jnp.einsum(
                "tkgd,skd->kgts", dout_heads, value_block, preferred_element_type=jnp.float32
            )
            score_grads = (attn_probs * (prob_grads - row_dots[..., None])).astype(jnp.bfloat16)
            dq_next = dq_now + jnp.einsum(
                "kgts,skd->tkgd", score_grads, key_block, preferred_element_type=jnp.float32
            )
            dk_block = (
                jnp.einsum(
                    "kgts,tkgd->skd", score_grads, q_heads, preferred_element_type=jnp.float32
                )
                * softmax_scale
            )
            return (dq_next, (dk_block, dv_block))

        def skip(dq_now):
            empty = jnp.zeros((block_len, kv_heads, HEAD_WIDTH), jnp.float32)
            return (dq_now, (empty, empty))

        return lax.cond(jnp.any(allowed_now), work, skip, dq_acc)

    start_dq = jnp.zeros(q_heads.shape, jnp.float32)
    dq_acc, (dk_blocks, dv_blocks) = lax.scan(
        grad_step, start_dq, (key_blocks, value_blocks, id_blocks, pos_blocks)
    )
    return (
        dq_acc * softmax_scale,
        dk_blocks.reshape(token_length, kv_heads, HEAD_WIDTH),
        dv_blocks.reshape(token_length, kv_heads, HEAD_WIDTH),
    )


def on_device(query, keys, values, output_gradient, forward_output, doc_ids):
    tok_rows = query.shape[1]
    kv_heads = keys.shape[2] // HEAD_WIDTH
    group_count = query.shape[2] // keys.shape[2]
    first_row = lax.axis_index("seq") * tok_rows
    all_keys, all_values, all_ids = (
        lax.all_gather(keys, "seq", axis=1, tiled=True),
        lax.all_gather(values, "seq", axis=1, tiled=True),
        lax.all_gather(doc_ids, "seq", axis=1, tiled=True),
    )
    token_length = all_ids.shape[1]
    q_heads = query[0].reshape(tok_rows, kv_heads, group_count, HEAD_WIDTH)
    dout_heads = output_gradient[0].reshape(tok_rows, kv_heads, group_count, HEAD_WIDTH)
    out_heads = forward_output[0].reshape(tok_rows, kv_heads, group_count, HEAD_WIDTH)
    key_rows = all_keys[0].reshape(token_length, kv_heads, HEAD_WIDTH)
    value_rows = all_values[0].reshape(token_length, kv_heads, HEAD_WIDTH)
    own_ids = doc_ids[0]
    key_ids = all_ids[0]
    grad_q, key_gradient, value_gradient = attend_grads(
        q_heads, dout_heads, out_heads, key_rows, value_rows, own_ids, key_ids, first_row
    )
    features = kv_heads * HEAD_WIDTH
    key_terms = key_gradient.reshape(1, token_length, features)
    value_terms = value_gradient.reshape(1, token_length, features)
    key_sums, value_sums = (
        lax.psum_scatter(key_terms, "seq", scatter_dimension=1, tiled=True),
        lax.psum_scatter(value_terms, "seq", scatter_dimension=1, tiled=True),
    )
    grad_query = grad_q.reshape(1, tok_rows, kv_heads * group_count * HEAD_WIDTH).astype(
        jnp.bfloat16
    )
    return (grad_query, key_sums.astype(jnp.bfloat16), value_sums.astype(jnp.bfloat16))


def solution(mesh):
    return jax.shard_map(
        on_device,
        mesh=mesh,
        in_specs=(
            P("dp", "seq", None),
            P("dp", "seq", None),
            P("dp", "seq", None),
            P("dp", "seq", None),
            P("dp", "seq", None),
            P("dp", "seq"),
        ),
        out_specs=(P("dp", "seq", None), P("dp", "seq", None), P("dp", "seq", None)),
        check_vma=False,
    )
```

profile of v0, /device:TPU:79, one launch (start us, length us, event | category | flops | bytes accessed | tf_op | source)
XLA Modules:
  0.0 395.5 jit_solution(2741356949223258458)
XLA Ops:
  8.7 20.7 %all_gather.9 = s32[1,4096]{1,0:T(1,128)S(1)} all-gather(s32[1,128]{1,0:T(1,128)} %param.19), channel_id=1, replica_groups=mesh['seq'=32,'dp'=4] {'seq'}, dimensions={1}, use_global_device_ids=true | all-gather | bytes 16896 | tf_op jit(solution)/shard_map/all_gather | solution.py:120
  35.4 20.8 %all-gather.3.cloned.1.call-done = bf16[1,4096,512]{2,1,0:T(8,128)(2,1)} async-done(((bf16[1,128,512]{2,1,0:T(8,128)(2,1)}), bf16[1,4096,512]{2,1,0:T(8,128)(2,1)}) %all-gather.3.cloned.1.call-update) | async-done | bytes 4194320 | tf_op jit(solution)/shard_map/all_gather | solution.py:118
  56.2 6.9 %reshape.51 = bf16[8,512,4,128]{3,2,1,0:T(4,128)(2,1)} reshape(bf16[1,4096,512]{2,1,0:T(8,128)(2,1)} %all-gather.3.cloned.1.call-done) | data formatting | bytes 8388608 | tf_op jit(solution)/shard_map/reshape;reshape;squeeze | solution.py:26
  63.1 5.2 %copy.21 = bf16[8,512,4,128]{3,1,2,0:T(8,128)(2,1)} copy(bf16[8,512,4,128]{3,2,1,0:T(4,128)(2,1)} %reshape.51) | data formatting | bytes 8388608
  68.3 17.1 %while.31 = (s32[]{:T(128)}, f32[4,4,128]{2,1,0:T(4,128)S(1)}, f32[4,4,128]{2,1,0:T(4,128)S(1)}, s32[8,512]{1,0:T(8,128)S(1)}, s32[1,128]{1,0:T(1,128)S(1)}, /*i...) while((s32[]{:T(128)}, f32[4,4,128]{2,1,0:T(4,128)S(1)}, ...), condition=%wide.region_6.7_spmd.clone, body=%wide.region_0.6_spmd.clone.sunk | while | flops 277090432 | bytes 9754827 | solution.py:64
  72.6 2.9 conditional.6
  72.6 1.8 fusion.4
  76.8 2.9 conditional.6
  76.9 1.8 fusion.4
  85.4 18.4 %all-gather.5.cloned.1.call-done = bf16[1,4096,512]{2,1,0:T(8,128)(2,1)} async-done(((bf16[1,128,512]{2,1,0:T(8,128)(2,1)}), bf16[1,4096,512]{2,1,0:T(8,128)(2,1)}) %all-gather.5.cloned.1.call-update) | async-done | bytes 4194320 | tf_op jit(solution)/shard_map/all_gather | solution.py:119
  103.9 6.9 %reshape.52 = bf16[8,512,4,128]{3,2,1,0:T(4,128)(2,1)} reshape(bf16[1,4096,512]{2,1,0:T(8,128)(2,1)} %all-gather.5.cloned.1.call-done) | data formatting | bytes 8388608 | tf_op jit(solution)/shard_map/reshape;reshape;squeeze | solution.py:27
  110.8 5.2 %copy.23 = bf16[8,512,4,128]{3,1,2,0:T(8,128)(2,1)} copy(bf16[8,512,4,128]{3,2,1,0:T(4,128)(2,1)} %reshape.52) | data formatting | bytes 8388608
  117.1 50.8 %while.32 = (s32[]{:T(128)}, f32[128,4,4,128]{3,0,2,1:T(8,128)}, f32[8,512,4,128]{3,2,1,0:T(4,128)}, f32[8,512,4,128]{3,2,1,0:T(4,128)}, s32[8,512]{1,0:T(8,128)...) while((s32[]{:T(128)}, f32[128,4,4,128]{3,0,2,1:T(8,128)}, ...), condition=%wide.region_12.13_spmd.clone, body=%wide.region_8.12_spmd.clone.sunk | while | flops 1353449600 | bytes 39558968 | solution.py:102
  118.8 2.6 copy_dynamic-update-slice_fusion.3
  123.2 2.7 copy_dynamic-update-slice_fusion.3
  127.4 8.1 %conditional.7 = (f32[128,4,4,128]{3,0,2,1:T(8,128)}, f32[1,512,4,128]{3,1,2,0:T(8,128)S(1)}, f32[1,512,4,128]{3,1,2,0:T(8,128)S(1)}) conditional(s32[]{:T(128)} %convert_element_type.73, f32[128,4,4,128]{3,0,2,1:T(8,128)} %get-tuple-element.607, (pred[128,512]{0,1:T(8,128)(4,1)S(1)}, bf16[8,512,4,128]{3,1,2,0:T(8,128)(2,1)}, s32[]{:T(128)}, ...), branch_computations={%region_10.10_spmd, %region_11.11_spmd} | conditional | flops 1353187328 | bytes 35284560 | solution.py:99
  127.4 1.8 fusion.28
  129.2 2.5 fusion.10
  131.6 2.3 fusion.23
  135.5 2.7 copy_dynamic-update-slice_fusion.3
  139.7 8.1 %conditional.7 = (f32[128,4,4,128]{3,0,2,1:T(8,128)}, f32[1,512,4,128]{3,1,2,0:T(8,128)S(1)}, f32[1,512,4,128]{3,1,2,0:T(8,128)S(1)}) conditional(s32[]{:T(128)} %convert_element_type.73, f32[128,4,4,128]{3,0,2,1:T(8,128)} %get-tuple-element.607, (pred[128,512]{0,1:T(8,128)(4,1)S(1)}, bf16[8,512,4,128]{3,1,2,0:T(8,128)(2,1)}, s32[]{:T(128)}, ...), branch_computations={%region_10.10_spmd, %region_11.11_spmd} | conditional | flops 1353187328 | bytes 35284560 | solution.py:99
  141.5 2.5 fusion.10
  143.9 2.3 fusion.23
  147.8 2.7 copy_dynamic-update-slice_fusion.3
  152.1 2.7 copy_dynamic-update-slice_fusion.3
  156.5 2.7 copy_dynamic-update-slice_fusion.3
  160.9 2.7 copy_dynamic-update-slice_fusion.3
  165.2 2.7 copy_dynamic-update-slice_fusion.3
  167.9 10.3 %reshape_reshape.6 = f32[1,4096,512]{2,1,0:T(8,128)} reshape(f32[8,512,4,128]{3,2,1,0:T(4,128)} %get-tuple-element.247) | data formatting | bytes 16777216 | tf_op jit(solution)/shard_map/reshape;reshape | solution.py:134
  178.2 10.3 %reshape_reshape.7 = f32[1,4096,512]{2,1,0:T(8,128)} reshape(f32[8,512,4,128]{3,2,1,0:T(4,128)} %get-tuple-element.248) | data formatting | bytes 16777216 | tf_op jit(solution)/shard_map/reshape;reshape | solution.py:135
  191.5 99.8 %reduce-scatter.3.cloned.1.call-done = f32[1,128,512]{2,1,0:T(8,128)} async-done(((f32[1,4096,512]{2,1,0:T(8,128)}), f32[1,128,512]{2,1,0:T(8,128)}) %reduce-scatter.3.cloned.1.call-update) | async-done | bytes 262160 | tf_op jit(solution)/shard_map/reduce_scatter | solution.py:137
  292.9 94.4 %reduce-scatter.5.cloned.1.call-done = f32[1,128,512]{2,1,0:T(8,128)} async-done(((f32[1,4096,512]{2,1,0:T(8,128)}), f32[1,128,512]{2,1,0:T(8,128)}) %reduce-scatter.5.cloned.1.call-update) | async-done | bytes 262160 | tf_op jit(solution)/shard_map/reduce_scatter | solution.py:138
  (134 shorter events, 37.0 us)
Async XLA Ops:
  7.2 49.1 %all-gather.3.cloned.1.call-start = ((), (), s32[]{:S(2)}) async-start(), calls=%async_computation.2 | async-start | bytes 4325376 | tf_op jit(solution)/shard_map/all_gather | solution.py:118
  7.9 96.0 %all-gather.5.cloned.1.call-start = ((), (), s32[]{:S(2)}) async-start(), calls=%async_computation.3 | async-start | bytes 4325376 | tf_op jit(solution)/shard_map/all_gather | solution.py:119
  8.6 282.6 %reduce-scatter.3.cloned.1.call-start = ((), (), s32[]{:S(2)}) async-start(), calls=%async_computation.4 | async-start | bytes 8650752 | tf_op jit(solution)/shard_map/reduce_scatter | solution.py:137
  63.1 5.2 %copy-start.3 = (s32[1,128]{1,0:T(1,128)S(1)}, s32[1,128]{1,0:T(1,128)}, u32[]{:S(2)}) copy-start(s32[1,128]{1,0:T(1,128)} %param.19) | copy-start | bytes 1540
  129.1 2.5 copy-start
  133.9 1.5 copy-start.1
  141.4 2.5 copy-start
  146.2 1.5 copy-start.1
  178.2 209.1 %reduce-scatter.5.cloned.1.call-start = ((), (), s32[]{:S(2)}) async-start(), calls=%async_computation.5 | async-start | bytes 8650752 | tf_op jit(solution)/shard_map/reduce_scatter | solution.py:138
  188.5 1.2 copy-start.2
Sparse Core Ops, SparseCore 0:
  10.3 45.9 all-gather.2
  58.5 45.3 all-gather.4
  178.3 112.9 reduce-scatter.2
  295.3 91.9 reduce-scatter.4
where the time goes:
time: 402 us; the launch traced here: 396 us
  waiting for transfers between devices  235 us (58%)
  local copies, waits for them, and re-layouts  76.1 us (19%)
  blocking collectives  20.7 us (5%)
  matrix products  19.6 us (5%)
  other arithmetic  19.5 us (5%)
  between operations  13.9 us (3%)
  loops' own time  10.7 us (3%)
    reduce_scatter x1, waiting for transfers between devices, on_device(): lax.psum_scatter(key_terms, 'seq', scatter_dimension=1, tiled=True)  99.8 us
    reduce_scatter x1, waiting for transfers between devices, on_device(): lax.psum_scatter(value_terms, 'seq', scatter_dimension=1, tiled=True)  94.4 us
    dynamic_update_slice x8, local copies, waits for them, and re-layouts, attend_grads(): lax.scan(grad_step, start_dq, (key_blocks, value_blocks, id_blocks, pos_b...  21.3 us
    all_gather x1, waiting for transfers between devices, on_device(): lax.all_gather(keys, 'seq', axis=1, tiled=True)  20.8 us
    all_gather x1, blocking collectives, on_device(): lax.all_gather(doc_ids, 'seq', axis=1, tiled=True)  20.7 us
    all_gather x1, waiting for transfers between devices, on_device(): lax.all_gather(values, 'seq', axis=1, tiled=True)  18.4 us
    unnamed x11, local copies, waits for them, and re-layouts  16.1 us
    another operation x1, local copies, waits for them, and re-layouts, on_device(): value_terms = value_gradient.reshape(1, token_length, features)  10.3 us
  transfers between devices with their start and end apart: 4, of which 4 were waited for; matrix products, arithmetic and copies ran while one was open for 11% of the time, Pallas kernels for 0%

commit v1 on v0

v1 whole, which is shorter than its diff:
```python
import functools
import math

import jax
import jax.numpy as jnp
from jax import lax
from jax.experimental import pallas as pl
from jax.experimental.pallas import tpu as pltpu
from jax.sharding import PartitionSpec as P

HEAD_WIDTH = 128
LONGEST = 2048
DOC_ROWS = 16
MASKED_LOW = -1e30
SCALE = 1.0 / math.sqrt(HEAD_WIDTH)
LOG2_E = math.log2(math.e)


def nn(a, b):
    return jnp.dot(a, b, preferred_element_type=jnp.float32)


def tn(a, b):
    return lax.dot_general(a, b, (((0,), (0,)), ((), ())), preferred_element_type=jnp.float32)


def kernel(
    chips, window, kv, group,
    q_ref, k_ref, v_ref, do_ref, o_ref, id_ref,
    dq_out, dk_out, dv_out,
    ksend, vsend, kbuf, vbuf, k_t,
    qsend, dosend, rdsend, qbuf, dobuf, rdbuf,
    q_h, q_t, do_h, do_t, rd_h,
    e_all, m_all, l_all, r_all,
    p_low, s_low, dq_t,
    psend, precv, diag, acc, dqsend, dqrecv,
    ks_sem, kr_sem, vs_sem, vr_sem, ps_sem, pr_sem, xs_sem, xr_sem,
):
    tok = q_ref.shape[0]
    span = 2 * tok
    heads = kv * group
    half = heads * HEAD_WIDTH
    kvf = kv * HEAD_WIDTH
    me = lax.axis_index("seq")
    chip = me // 2
    core = me % 2
    other = 1 - core
    partner = chip * 2 + other
    n_back = jnp.minimum(chip, window)
    n_fwd = jnp.minimum(chips - 1 - chip, window)

    barrier = pltpu.get_barrier_semaphore()
    pl.semaphore_signal(barrier, inc=1, device_id={"seq": partner})

    def greet_back(o, c):
        for side in range(2):
            pl.semaphore_signal(barrier, inc=1, device_id={"seq": (chip - o) * 2 + side})
        return c

    def greet_fwd(o, c):
        for side in range(2):
            pl.semaphore_signal(barrier, inc=1, device_id={"seq": (chip + o) * 2 + side})
        return c

    lax.fori_loop(1, n_back + 1, greet_back, 0)
    lax.fori_loop(1, n_fwd + 1, greet_fwd, 0)

    ids = id_ref[...]
    rows = lax.broadcasted_iota(jnp.int32, (DOC_ROWS, tok), 0)
    onehot = jnp.where(rows == ids, 1.0, 0.0).astype(jnp.bfloat16)
    for side in range(2):
        ksend[side, :tok, :] = k_ref[:, side * kvf:(side + 1) * kvf]
        ksend[side, tok:, :tok] = onehot
        ksend[side, tok:, tok:] = jnp.zeros((DOC_ROWS, kvf - tok), jnp.bfloat16)
        vsend[side] = v_ref[:, side * kvf:(side + 1) * kvf]
    kbuf[0, core] = ksend[core]
    vbuf[0, core] = vsend[core]
    own_cols = pl.ds(pl.multiple_of(core * half, half), half)
    other_cols = pl.ds(pl.multiple_of(other * half, half), half)
    qsend[...] = q_ref[:, other_cols]
    dosend[...] = do_ref[:, other_cols]
    qbuf[core] = q_ref[:, own_cols]
    dobuf[core] = do_ref[:, own_cols]

    pl.semaphore_wait(barrier, 1 + 2 * (n_back + n_fwd))

    def swap(src, dst, slot):
        return pltpu.make_async_remote_copy(
            src_ref=src, dst_ref=dst, send_sem=xs_sem.at[slot], recv_sem=xr_sem.at[slot],
            device_id={"seq": partner},
        )

    def k_copy(o, side, slot_side, target):
        return pltpu.make_async_remote_copy(
            src_ref=ksend.at[side], dst_ref=kbuf.at[o, slot_side],
            send_sem=ks_sem.at[o, side], recv_sem=kr_sem.at[o, slot_side],
            device_id={"seq": target},
        )

    def v_copy(o, side, slot_side, target):
        return pltpu.make_async_remote_copy(
            src_ref=vsend.at[side], dst_ref=vbuf.at[o, slot_side],
            send_sem=vs_sem.at[o, side], recv_sem=vr_sem.at[o, slot_side],
            device_id={"seq": target},
        )

    def p_copy(o, side, slot_side, target):
        return pltpu.make_async_remote_copy(
            src_ref=psend.at[o, side], dst_ref=precv.at[o, slot_side],
            send_sem=ps_sem.at[o, side], recv_sem=pr_sem.at[o, slot_side],
            device_id={"seq": target},
        )

    q_swap = swap(qsend, qbuf.at[core], 0)
    do_swap = swap(dosend, dobuf.at[core], 1)
    rd_swap = swap(rdsend, rdbuf.at[core], 2)
    dq_swap = swap(dqsend, dqrecv, 3)
    q_swap.start()
    k_copy(0, other, core, partner).start()

    def send_k(o, c):
        for side in range(2):
            k_copy(o, side, core, (chip + o) * 2 + side).start()
        return c

    def send_v(o, c):
        for side in range(2):
            v_copy(o, side, core, (chip + o) * 2 + side).start()
        return c

    lax.fori_loop(1, n_fwd + 1, send_k, 0)
    do_swap.start()
    v_copy(0, other, core, partner).start()
    lax.fori_loop(1, n_fwd + 1, send_v, 0)

    def dots_of(cols):
        prod = do_ref[:, cols].astype(jnp.float32) * o_ref[:, cols].astype(jnp.float32)
        return jnp.sum(jnp.transpose(prod), axis=0, keepdims=True)

    for h in range(heads):
        rdsend[h:h + 1, :] = dots_of(
            pl.ds(pl.multiple_of(other * half + h * HEAD_WIDTH, HEAD_WIDTH), HEAD_WIDTH))
        rdbuf[core, h:h + 1, :] = dots_of(
            pl.ds(pl.multiple_of(core * half + h * HEAD_WIDTH, HEAD_WIDTH), HEAD_WIDTH))
    rd_swap.start()

    swap(qsend, qbuf.at[other], 0).wait_recv()
    for h in range(heads):
        cols = slice(h * HEAD_WIDTH, (h + 1) * HEAD_WIDTH)
        both = jnp.concatenate([qbuf[0, :, cols], qbuf[1, :, cols]], axis=0)
        q_h[h // group, (h % group) * span:(h % group + 1) * span, :] = both
        q_t[:, h * span:(h + 1) * span] = jnp.transpose(both)
    k_copy(0, other, other, partner).wait_recv()
    onehot_q = jnp.concatenate(
        [kbuf[0, 0, tok:, :tok], kbuf[0, 1, tok:, :tok]], axis=1)

    def stats(o, c):
        @pl.when(o > 0)
        def _():
            for side in range(2):
                k_copy(o, side, side, partner).wait_recv()

        onehot_k = jnp.concatenate([kbuf[o, 0, tok:, :tok], kbuf[o, 1, tok:, :tok]], axis=1)
        same = tn(onehot_k, onehot_q)
        key_pos = lax.broadcasted_iota(jnp.int32, (span, span), 0)
        query_pos = lax.broadcasted_iota(jnp.int32, (span, span), 1)
        allowed = (same > 0.5) & (key_pos <= query_pos + o * span)
        bias = jnp.where(allowed, 0.0, MASKED_LOW)
        for j in range(kv):
            cols = slice(j * HEAD_WIDTH, (j + 1) * HEAD_WIDTH)
            k_j = jnp.concatenate([kbuf[o, 0, :tok, cols], kbuf[o, 1, :tok, cols]], axis=0)
            k_t[o, j] = jnp.transpose(k_j)
            for g in range(group):
                h = j * group + g
                s = nn(k_j, q_t[:, h * span:(h + 1) * span]) * (SCALE * LOG2_E) + bias
                m = jnp.max(s, axis=0, keepdims=True)
                e = jnp.exp2(s - m)
                e_all[o, h] = e
                m_all[o, h:h + 1, :] = m
                l_all[o, h:h + 1, :] = jnp.sum(e, axis=0, keepdims=True)
        return c

    lax.fori_loop(0, n_back + 1, stats, 0)

    m_top = lax.fori_loop(1, n_back + 1, lambda o, m: jnp.maximum(m, m_all[o]), m_all[0])
    total = lax.fori_loop(
        0, n_back + 1, lambda o, t: t + l_all[o] * jnp.exp2(m_all[o] - m_top),
        jnp.zeros((heads, span), jnp.float32))
    inverse = 1.0 / total

    def ratios(o, c):
        r_all[o] = jnp.exp2(m_all[o] - m_top) * inverse
        return c

    lax.fori_loop(0, n_back + 1, ratios, 0)

    swap(dosend, dobuf.at[other], 1).wait_recv()
    swap(rdsend, rdbuf.at[other], 2).wait_recv()
    for h in range(heads):
        cols = slice(h * HEAD_WIDTH, (h + 1) * HEAD_WIDTH)
        both = jnp.concatenate([dobuf[0, :, cols], dobuf[1, :, cols]], axis=0)
        do_h[h // group, (h % group) * span:(h % group + 1) * span, :] = both
        do_t[:, h * span:(h + 1) * span] = jnp.transpose(both)
    rd_h[...] = jnp.concatenate([rdbuf[0], rdbuf[1]], axis=1)
    dq_t[...] = jnp.zeros(dq_t.shape, jnp.float32)
    v_copy(0, other, other, partner).wait_recv()

    def grads(step, c):
        o = n_back - step

        @pl.when(o > 0)
        def _():
            for side in range(2):
                v_copy(o, side, side, partner).wait_recv()

        for j in range(kv):
            cols = slice(j * HEAD_WIDTH, (j + 1) * HEAD_WIDTH)
            v_j = jnp.concatenate([vbuf[o, 0, :, cols], vbuf[o, 1, :, cols]], axis=0)
            for g in range(group):
                h = j * group + g
                dp = nn(v_j, do_t[:, h * span:(h + 1) * span])
                p = e_all[o, h] * r_all[o, h:h + 1, :]
                ds = p * (dp - rd_h[h:h + 1, :])
                p_low[j, :, g * span:(g + 1) * span] = p.astype(jnp.bfloat16)
                s_low[j, :, g * span:(g + 1) * span] = ds.astype(jnp.bfloat16)
            dv = nn(p_low[j], do_h[j])
            dk = nn(s_low[j], q_h[j]) * SCALE
            dq_t[j] += nn(k_t[o, j], s_low[j])
            for side in range(2):
                piece = slice(side * tok, (side + 1) * tok)
                psend[o, side, 0, :, cols] = dk[piece].astype(jnp.bfloat16)
                psend[o, side, 1, :, cols] = dv[piece].astype(jnp.bfloat16)

            @pl.when(o == 0)
            def _():
                for side in range(2):
                    piece = slice(side * tok, (side + 1) * tok)
                    diag[side, 0, :, cols] = dk[piece]
                    diag[side, 1, :, cols] = dv[piece]

        @pl.when(o > 0)
        def _():
            for side in range(2):
                p_copy(o, side, core, (chip - o) * 2 + side).start()

        return c

    lax.fori_loop(0, n_back + 1, grads, 0)
    p_copy(0, other, core, partner).start()

    for h in range(heads):
        cols = slice(h * HEAD_WIDTH, (h + 1) * HEAD_WIDTH)
        piece = jnp.transpose(
            dq_t[h // group, :, (h % group) * span:(h % group + 1) * span] * SCALE
        ).astype(jnp.bfloat16)
        dobuf[0, :, cols] = piece[:tok]
        dobuf[1, :, cols] = piece[tok:]
    dqsend[...] = dobuf[other]
    dq_swap.start()
    dq_out[:, own_cols] = dobuf[core]

    acc[core] = diag[core]
    p_copy(0, other, other, partner).wait_recv()
    acc[other] = precv[0, other].astype(jnp.float32)

    def collect(o, c):
        for side in range(2):
            p_copy(o, side, side, partner).wait_recv()
            acc[side] += precv[o, side].astype(jnp.float32)
        return c

    lax.fori_loop(1, n_fwd + 1, collect, 0)
    for side in range(2):
        cols = slice(side * kvf, (side + 1) * kvf)
        dk_out[:, cols] = acc[side, 0].astype(jnp.bfloat16)
        dv_out[:, cols] = acc[side, 1].astype(jnp.bfloat16)
    dq_swap.wait_recv()
    dq_out[:, other_cols] = dqrecv[...]

    q_swap.wait_send()
    do_swap.wait_send()
    rd_swap.wait_send()
    dq_swap.wait_send()
    k_copy(0, other, core, partner).wait_send()
    v_copy(0, other, core, partner).wait_send()
    p_copy(0, other, core, partner).wait_send()

    def sent_fwd(o, c):
        for side in range(2):
            k_copy(o, side, core, partner).wait_send()
            v_copy(o, side, core, partner).wait_send()
        return c

    def sent_back(o, c):
        for side in range(2):
            p_copy(o, side, core, partner).wait_send()
        return c

    lax.fori_loop(1, n_fwd + 1, sent_fwd, 0)
    lax.fori_loop(1, n_back + 1, sent_back, 0)


def on_device(seq_size, query, keys, values, output_gradient, forward_output, doc_ids):
    tok = query.shape[1]
    span = 2 * tok
    chips = seq_size // 2
    window = min(-(-LONGEST // span), chips - 1)
    kv = keys.shape[2] // HEAD_WIDTH // 2
    group = query.shape[2] // keys.shape[2]
    heads = kv * group
    half = heads * HEAD_WIDTH
    kvf = kv * HEAD_WIDTH
    slots = window + 1
    bf, f32 = jnp.bfloat16, jnp.float32
    vmem = pl.BlockSpec(memory_space=pltpu.VMEM)
    dma = pltpu.SemaphoreType.DMA
    grad_query, grad_keys, grad_values = pl.pallas_call(
        functools.partial(kernel, chips, window, kv, group),
        out_shape=(
            jax.ShapeDtypeStruct((tok, 2 * half), bf),
            jax.ShapeDtypeStruct((tok, 2 * kvf), bf),
            jax.ShapeDtypeStruct((tok, 2 * kvf), bf),
        ),
        in_specs=[vmem] * 6,
        out_specs=(vmem,) * 3,
        scratch_shapes=[
            pltpu.VMEM((2, tok + DOC_ROWS, kvf), bf),
            pltpu.VMEM((2, tok, kvf), bf),
            pltpu.VMEM((slots, 2, tok + DOC_ROWS, kvf), bf),
            pltpu.VMEM((slots, 2, tok, kvf), bf),
            pltpu.VMEM((slots, kv, HEAD_WIDTH, span), bf),
            pltpu.VMEM((tok, half), bf),
            pltpu.VMEM((tok, half), bf),
            pltpu.VMEM((heads, tok), f32),
            pltpu.VMEM((2, tok, half), bf),
            pltpu.VMEM((2, tok, half), bf),
            pltpu.VMEM((2, heads, tok), f32),
            pltpu.VMEM((kv, group * span, HEAD_WIDTH), bf),
            pltpu.VMEM((HEAD_WIDTH, heads * span), bf),
            pltpu.VMEM((kv, group * span, HEAD_WIDTH), bf),
            pltpu.VMEM((HEAD_WIDTH, heads * span), bf),
            pltpu.VMEM((heads, span), f32),
            pltpu.VMEM((slots, heads, span, span), f32),
            pltpu.VMEM((slots, heads, span), f32),
            pltpu.VMEM((slots, heads, span), f32),
            pltpu.VMEM((slots, heads, span), f32),
            pltpu.VMEM((kv, span, group * span), bf),
            pltpu.VMEM((kv, span, group * span), bf),
            pltpu.VMEM((kv, HEAD_WIDTH, group * span), f32),
            pltpu.VMEM((slots, 2, 2, tok, kvf), bf),
            pltpu.VMEM((slots, 2, 2, tok, kvf), bf),
            pltpu.VMEM((2, 2, tok, kvf), f32),
            pltpu.VMEM((2, 2, tok, kvf), f32),
            pltpu.VMEM((tok, half), bf),
            pltpu.VMEM((tok, half), bf),
            dma((slots, 2)), dma((slots, 2)), dma((slots, 2)), dma((slots, 2)),
            dma((slots, 2)), dma((slots, 2)), dma((4,)), dma((4,)),
        ],
        compiler_params=pltpu.CompilerParams(
            collective_id=0, has_side_effects=True, vmem_limit_bytes=56 * 1024 * 1024,
        ),
    )(query[0], keys[0], values[0], output_gradient[0], forward_output[0], doc_ids)
    return grad_query[None], grad_keys[None], grad_values[None]


def solution(mesh):
    wide = P("dp", "seq", None)
    return jax.shard_map(
        functools.partial(on_device, mesh.shape["seq"]),
        mesh=mesh,
        in_specs=(wide, wide, wide, wide, wide, P("dp", "seq")),
        out_specs=(wide, wide, wide),
        check_vma=False,
    )
```

time: 402 us -> 92.3 us (0.23)
  the two profiles are of different devices: /device:TPU:79 before, /device:TPU:77 now
where the time goes in v1:
time: 92.3 us; the launch traced here: 92.1 us
  Pallas kernels  88 us (95%)
  local copies, waits for them, and re-layouts  3.53 us (4%)
    pallas_call x1, Pallas kernels, on_device(): pl.pallas_call(functools.partial(kernel, chips, window, kv, group), out_s...  88 us
    unnamed x7, local copies, waits for them, and re-layouts  3.53 us

profile of v1, /device:TPU:77, one launch (start us, length us, event | category | flops | bytes accessed | tf_op | source)
XLA Modules:
  0.0 92.1 jit_solution(7768293934914023655)
XLA Ops:
  0.6 88.0 %shard_map.85 = (bf16[128,2048]{1,0:T(8,128)(2,1)}, bf16[128,512]{1,0:T(8,128)(2,1)}, bf16[128,512]{1,0:T(8,128)(2,1)}) custom-call(bf16[128,2048]{1,0:T(8,128)(2,1)} %bitcast.9, bf16[128,512]{1,0:T(8,128)(2,1)} %bitcast.14, bf16[128,512]{1,0:T(8,128)(2,1)} %bitcast.15, bf16[128,2048]{1,0:T(8,128)(2,1)} %bitcast.10, bf16[128,2048]{1,0:T(8,128)(2,1)} %bitcast.11, ...), custom_call_target="tpu_custom_call" | custom-call | tf_op jit(solution)/shard_map/pallas_call | solution.py:317
  88.6 0.0 copy-start.1
  88.6 1.9 %copy.12 = bf16[1,128,2048]{2,1,0:T(8,128)(2,1)} copy(bf16[1,128,2048]{2,1,0:T(8,128)(2,1)} %bitcast.8) | data formatting | bytes 1048576
  90.5 0.0 copy-done.1
  90.5 0.0 copy-start
  90.5 0.7 copy.13
  91.2 0.3 copy-done
  91.5 0.7 copy.14
Async XLA Ops:
  88.6 1.9 %copy-start.1 = (bf16[128,512]{1,0:T(8,128)(2,1)S(1)}, bf16[128,512]{1,0:T(8,128)(2,1)}, u32[]{:S(2)}) copy-start(bf16[128,512]{1,0:T(8,128)(2,1)} %get-tuple-element.7) | copy-start | bytes 393220
  90.5 1.0 %copy-start = (bf16[128,512]{1,0:T(8,128)(2,1)S(1)}, bf16[128,512]{1,0:T(8,128)(2,1)}, u32[]{:S(2)}) copy-start(bf16[128,512]{1,0:T(8,128)(2,1)} %get-tuple-element.8) | copy-start | bytes 393220

commit v2 on v0

v2 whole, which is shorter than its diff:
```python
import functools
import math

import jax
import jax.numpy as jnp
from jax import lax
from jax.experimental import pallas as pl
from jax.experimental.pallas import tpu as pltpu
from jax.sharding import PartitionSpec as P

HEAD_WIDTH = 128
LONGEST = 2048
DOC_ROWS = 16
MASKED_LOW = -1e30
SCALE = 1.0 / math.sqrt(HEAD_WIDTH)
LOG2_SCALE = SCALE * math.log2(math.e)
CHIPS = 4
PAIR = 2
REMOTE = (1, 3, 2)


def nn(a, b):
    return jnp.dot(a, b, preferred_element_type=jnp.float32)


def kernel(
    rows, back,
    q_ref, k_ref, v_ref, do_ref, o_ref, id_ref,
    dq_out, dk_out, dv_out,
    ksend, kbuf, vbuf, k_x, k_t,
    rdsend, qbuf, dobuf, rdbuf, q_x, q_h, do_t, do_h, rd_h,
    e_all, m_all, l_all, r_all, dq_t,
    kv_acc, xrecv, ysend, yrecv, fsend, frecv, dqsend, dqrecv,
    ks, kr, vs, vr, qs, qr, gs, gr, rs, rr,
    kps, kpr, vps, vpr, kys, kyr, vys, vyr,
    xs, xr, ys, yr, fs, fr, ds, dr,
):
    tok = q_ref.shape[0]
    span = 2 * tok
    width = PAIR * HEAD_WIDTH
    hw = HEAD_WIDTH
    me = lax.axis_index("seq")
    core = me % 2
    other = 1 - core
    x = (me // 2) % CHIPS
    y = me // (2 * CHIPS)
    depth = jnp.minimum(y, back)
    reach = jnp.minimum(rows - 1 - y, back)

    def at(row, col, side):
        return {"seq": (row * CHIPS + col) * 2 + side}

    def turn(dx):
        return (x + dx) % CHIPS

    partner = at(y, x, other)

    barrier = pltpu.get_barrier_semaphore()
    pl.semaphore_signal(barrier, inc=1, device_id=partner)
    for dx in REMOTE:
        for side in range(2):
            pl.semaphore_signal(barrier, inc=1, device_id=at(y, turn(dx), side))

    def greet_back(r, c):
        pl.semaphore_signal(barrier, inc=1, device_id=at(y - r, x, core))
        return c

    def greet_fwd(r, c):
        pl.semaphore_signal(barrier, inc=1, device_id=at(y + r, x, core))
        return c

    lax.fori_loop(1, depth + 1, greet_back, 0)
    lax.fori_loop(1, reach + 1, greet_fwd, 0)

    def feats(head, count):
        return pl.ds(pl.multiple_of(head * hw, hw), count * hw)

    def pair_cols(col, side):
        return feats(col * 2 * PAIR + side * PAIR, PAIR)

    doc_rows = lax.broadcasted_iota(jnp.int32, (DOC_ROWS, tok), 0)
    barred = jnp.where(doc_rows == id_ref[...], 0.0, MASKED_LOW).astype(jnp.bfloat16)
    for col in range(CHIPS):
        ksend[col, :tok, :] = k_ref[:, col * hw:(col + 1) * hw]
        ksend[col, tok:, :] = barred
    kbuf[core, x] = ksend[x]
    vbuf[core, x] = v_ref[:, feats(x, 1)]
    qbuf[x, core] = q_ref[:, pair_cols(x, core)]
    dobuf[x, core] = do_ref[:, pair_cols(x, core)]

    pl.semaphore_wait(barrier, 2 * CHIPS - 1 + depth + reach)

    def remote(src, dst, send, recv, target):
        return pltpu.make_async_remote_copy(
            src_ref=src, dst_ref=dst, send_sem=send, recv_sem=recv, device_id=target)

    def k_copy(dx):
        return remote(ksend.at[turn(dx)], kbuf.at[core, x], ks.at[dx], kr.at[x],
                      at(y, turn(dx), core))

    def v_copy(dx):
        return remote(v_ref.at[:, feats(turn(dx), 1)], vbuf.at[core, x], vs.at[dx], vr.at[x],
                      at(y, turn(dx), core))

    def q_copy(dx, side):
        return remote(q_ref.at[:, pair_cols(turn(dx), side)], qbuf.at[x, core],
                      qs.at[dx, side], qr.at[x, core], at(y, turn(dx), side))

    def do_copy(dx, side):
        return remote(do_ref.at[:, pair_cols(turn(dx), side)], dobuf.at[x, core],
                      gs.at[dx, side], gr.at[x, core], at(y, turn(dx), side))

    def rd_copy(dx, side):
        return remote(rdsend.at[turn(dx), side], rdbuf.at[x, core],
                      rs.at[dx, side], rr.at[x, core], at(y, turn(dx), side))

    def k_from(col):
        return remote(ksend.at[0], kbuf.at[core, col], ks.at[0], kr.at[col], partner)

    def v_from(col):
        return remote(v_ref.at[:, :hw], vbuf.at[core, col], vs.at[0], vr.at[col], partner)

    def q_from(col, side):
        return remote(q_ref.at[:, :width], qbuf.at[col, side], qs.at[0, 0], qr.at[col, side],
                      partner)

    def do_from(col, side):
        return remote(do_ref.at[:, :width], dobuf.at[col, side], gs.at[0, 0], gr.at[col, side],
                      partner)

    def rd_from(col, side):
        return remote(rdsend.at[0, 0], rdbuf.at[col, side], rs.at[0, 0], rr.at[col, side], partner)

    def row_of(r):
        return pl.ds(r * CHIPS, CHIPS)

    def k_pass(r, side):
        return remote(kbuf.at[side, row_of(r)], kbuf.at[side, row_of(r)], kps.at[r], kpr.at[r],
                      partner)

    def v_pass(r, side):
        return remote(vbuf.at[side, row_of(r)], vbuf.at[side, row_of(r)], vps.at[r], vpr.at[r],
                      partner)

    def k_row(r):
        return remote(kbuf.at[core, row_of(0)], kbuf.at[core, row_of(r)], kys.at[r], kyr.at[r],
                      at(y + r, x, core))

    def v_row(r):
        return remote(vbuf.at[core, row_of(0)], vbuf.at[core, row_of(r)], vys.at[r], vyr.at[r],
                      at(y + r, x, core))

    for dx in REMOTE:
        k_copy(dx).start()
    q_copy(0, other).start()
    for dx in REMOTE:
        for side in range(2):
            q_copy(dx, side).start()
    for dx in REMOTE:
        v_copy(dx).start()
    do_copy(0, other).start()
    for dx in REMOTE:
        for side in range(2):
            do_copy(dx, side).start()

    for col in range(CHIPS):
        for side in range(2):
            for g in range(PAIR):
                h = (col * 2 + side) * PAIR + g
                cols = slice(h * hw, (h + 1) * hw)
                prod = do_ref[:, cols].astype(jnp.float32) * o_ref[:, cols].astype(jnp.float32)
                rdsend[col, side, g:g + 1, :] = jnp.sum(
                    jnp.transpose(prod), axis=0, keepdims=True)
            rdsend[col, side, PAIR:, :] = jnp.zeros((8 - PAIR, tok), jnp.float32)
    rdbuf[x, core] = rdsend[x, core]
    rd_copy(0, other).start()
    for dx in REMOTE:
        for side in range(2):
            rd_copy(dx, side).start()

    def start_k_row(r, c):
        k_row(r).start()
        return c

    def start_v_row(r, c):
        v_row(r).start()
        return c

    def build_keys(r):
        def one(i, c):
            slot = r * CHIPS + i
            both = jnp.concatenate([kbuf[0, slot, :tok, :], kbuf[1, slot, :tok, :]], axis=0)
            bars = jnp.concatenate([kbuf[0, slot, tok:, :], kbuf[1, slot, tok:, :]], axis=1)
            pad = jnp.zeros((hw - DOC_ROWS, span), jnp.bfloat16)
            k_x[slot, :, :hw] = both
            k_x[slot, :, hw:] = jnp.transpose(jnp.concatenate([bars, pad], axis=0))
            k_t[slot] = jnp.transpose(both)
            return c

        lax.fori_loop(0, CHIPS, one, 0)

    for dx in REMOTE:
        k_from(turn(dx)).wait_recv()
    k_pass(0, core).start()
    lax.fori_loop(1, reach + 1, start_k_row, 0)
    k_pass(0, other).wait_recv()
    build_keys(0)

    def order(i):
        return (x + i + i // 2 - 2 * (i // 3)) % CHIPS

    def first_row(r, c):
        @pl.when(r > 0)
        def _():
            remote(kbuf.at[core, row_of(0)], kbuf.at[core, row_of(r)], kys.at[r], kyr.at[r],
                   partner).wait_recv()
            k_pass(r, core).start()
            k_pass(r, other).wait_recv()
            build_keys(r)

        def first_chunk(i, c):
            qc = order(i)

            @pl.when(r == 0)
            def _():
                for side in range(2):
                    @pl.when((qc != x) | (core != side))
                    def _():
                        q_from(qc, side).wait_recv()
                for g in range(PAIR):
                    cols = slice(g * hw, (g + 1) * hw)
                    both = jnp.concatenate([qbuf[qc, 0, :, cols], qbuf[qc, 1, :, cols]], axis=0)
                    q_h[qc, g * span:(g + 1) * span, :] = both
                    q_x[qc, :hw, g * span:(g + 1) * span] = jnp.transpose(both)
                    for side in range(2):
                        start = g * span + side * tok
                        bars = kbuf[side, qc, tok:, :].astype(jnp.float32)
                        q_x[qc, hw:hw + DOC_ROWS, start:start + tok] = jnp.where(
                            bars == 0.0, 1.0, 0.0).astype(jnp.bfloat16)
                q_x[qc, hw + DOC_ROWS:, :] = jnp.zeros(
                    (hw - DOC_ROWS, PAIR * span), jnp.bfloat16)

            def tile(kc, c):
                o = r * CHIPS + qc - kc
                place = qc * (back * CHIPS + 1) + o

                def finish(s):
                    m = jnp.max(s, axis=0, keepdims=True)
                    e = jnp.exp2((s - m) * LOG2_SCALE)
                    e_all[place] = e
                    m_all[place] = m
                    l_all[place] = jnp.sum(e, axis=0, keepdims=True)

                @pl.when(o > 0)
                def _():
                    finish(nn(k_x[r * CHIPS + kc], q_x[qc]))

                @pl.when(o == 0)
                def _():
                    s = nn(k_x[r * CHIPS + kc], q_x[qc])
                    key_pos = lax.broadcasted_iota(jnp.int32, (span, PAIR * span), 0)
                    query_pos = lax.broadcasted_iota(jnp.int32, (span, PAIR * span), 1) % span
                    finish(jnp.where(key_pos <= query_pos, s, MASKED_LOW))

                return c

            low = jnp.where(r == back, qc, 0)
            high = jnp.where(r == 0, qc + 1, CHIPS)
            lax.fori_loop(low, high, tile, 0)
            return c

        lax.fori_loop(0, CHIPS, first_chunk, 0)

        @pl.when(r == 0)
        def _():
            for dx in REMOTE:
                v_from(turn(dx)).wait_recv()
            v_pass(0, core).start()
            lax.fori_loop(1, reach + 1, start_v_row, 0)

        return c

    lax.fori_loop(0, depth + 1, first_row, 0)

    v_pass(0, other).wait_recv()

    def take_values(r, c):
        remote(vbuf.at[core, row_of(0)], vbuf.at[core, row_of(r)], vys.at[r], vyr.at[r],
               partner).wait_recv()
        v_pass(r, core).start()
        return c

    def have_values(r, c):
        v_pass(r, other).wait_recv()
        return c

    lax.fori_loop(1, depth + 1, take_values, 0)

    def ready(i, c):
        qc = order(i)
        base = qc * (back * CHIPS + 1)
        last = jnp.minimum(y * CHIPS + qc, back * CHIPS)
        m_top = lax.fori_loop(
            1, last + 1, lambda o, m: jnp.maximum(m, m_all[base + o]), m_all[base])
        total = lax.fori_loop(
            0, last + 1,
            lambda o, t: t + l_all[base + o] * jnp.exp2((m_all[base + o] - m_top) * LOG2_SCALE),
            jnp.zeros((1, PAIR * span), jnp.float32))
        inverse = 1.0 / total

        def ratio(o, c):
            r_all[base + o] = jnp.exp2((m_all[base + o] - m_top) * LOG2_SCALE) * inverse
            return c

        lax.fori_loop(0, last + 1, ratio, 0)
        for side in range(2):
            @pl.when((qc != x) | (core != side))
            def _():
                do_from(qc, side).wait_recv()
                rd_from(qc, side).wait_recv()
        for g in range(PAIR):
            cols = slice(g * hw, (g + 1) * hw)
            both = jnp.concatenate([dobuf[qc, 0, :, cols], dobuf[qc, 1, :, cols]], axis=0)
            do_h[qc, g * span:(g + 1) * span, :] = both
            do_t[qc, :, g * span:(g + 1) * span] = jnp.transpose(both)
            for side in range(2):
                start = g * span + side * tok
                rd_h[qc, :, start:start + tok] = rdbuf[qc, side, g:g + 1, :]
        dq_t[qc] = jnp.zeros((hw, PAIR * span), jnp.float32)
        return c

    lax.fori_loop(0, CHIPS, ready, 0)
    lax.fori_loop(1, depth + 1, have_values, 0)

    def x_copy(slot):
        return remote(kv_acc.at[slot, other], xrecv.at[slot], xs.at[slot], xr.at[slot], partner)

    def y_copy(r, kc):
        return remote(ysend.at[r - 1, kc], yrecv.at[r - 1, kc], ys.at[r - 1, kc],
                      yr.at[r - 1, kc], at(y - r, x, core))

    def dq_copy(col, side):
        return remote(dqsend.at[col, side], dqrecv.at[x, core], ds.at[col, side],
                      dr.at[x, core], at(y, col, side))

    def settle(n):
        r = depth - n // CHIPS
        kc = n % CHIPS
        slot = r * CHIPS + kc
        x_copy(slot).wait_recv()
        kv_sum = kv_acc[slot, core] + xrecv[slot]

        @pl.when(r > 0)
        def _():
            ysend[r - 1, kc] = kv_sum.astype(jnp.bfloat16)
            y_copy(r, kc).start()

        @pl.when(r == 0)
        def _():
            xrecv[slot] = kv_sum

    def second(n, c):
        r = depth - n // CHIPS
        kc = n % CHIPS
        slot = r * CHIPS + kc
        v_both = jnp.concatenate([vbuf[0, slot], vbuf[1, slot]], axis=0)

        def tile(qc, sums):
            dk, dv = sums
            place = qc * (back * CHIPS + 1) + r * CHIPS + qc - kc
            dp = nn(v_both, do_t[qc])
            p = e_all[place] * r_all[place]
            p_low = p.astype(jnp.bfloat16)
            s_low = (p * (dp - rd_h[qc])).astype(jnp.bfloat16)
            dq_t[qc] += nn(k_t[slot], s_low)
            return dk + nn(s_low, q_h[qc]), dv + nn(p_low, do_h[qc])

        low = jnp.where(r == 0, kc, 0)
        high = jnp.where(r == back, kc + 1, CHIPS)
        zero = jnp.zeros((span, hw), jnp.float32)
        dk, dv = lax.fori_loop(low, high, tile, (zero, zero))
        dk = dk * SCALE
        for side in range(2):
            kv_acc[slot, side, 0] = dk[side * tok:(side + 1) * tok]
            kv_acc[slot, side, 1] = dv[side * tok:(side + 1) * tok]
        x_copy(slot).start()

        @pl.when(n > 0)
        def _():
            settle(n - 1)

        @pl.when(r == 0)
        def _():
            for g in range(PAIR):
                cols = slice(g * hw, (g + 1) * hw)
                piece = jnp.transpose(
                    dq_t[kc, :, g * span:(g + 1) * span] * SCALE).astype(jnp.bfloat16)
                dqsend[kc, 0, :, cols] = piece[:tok]
                dqsend[kc, 1, :, cols] = piece[tok:]
            for side in range(2):
                @pl.when((kc != x) | (core != side))
                def _():
                    dq_copy(kc, side).start()

        return c

    blocks = (depth + 1) * CHIPS
    lax.fori_loop(0, blocks, second, 0)
    settle(blocks - 1)

    def f_copy(col):
        return remote(fsend.at[col], frecv.at[x], fs.at[col], fr.at[x], at(y, col, core))

    def deliver(kc, c):
        def more(r, t):
            remote(ysend.at[0, 0], yrecv.at[r - 1, kc], ys.at[0, 0], yr.at[r - 1, kc],
                   partner).wait_recv()
            return t + yrecv[r - 1, kc].astype(jnp.float32)

        fsend[kc] = lax.fori_loop(1, reach + 1, more, xrecv[kc]).astype(jnp.bfloat16)

        @pl.when(kc != x)
        def _():
            f_copy(kc).start()

        return c

    lax.fori_loop(0, CHIPS, deliver, 0)

    frecv[x] = fsend[x]
    dqrecv[x, core] = dqsend[x, core]
    dq_from = lambda col, side: remote(
        dqsend.at[0, 0], dqrecv.at[col, side], ds.at[0, 0], dr.at[col, side], partner)
    dq_from(x, other).wait_recv()
    for dx in REMOTE:
        for side in range(2):
            dq_from(turn(dx), side).wait_recv()
    for col in range(CHIPS):
        for side in range(2):
            start = (col * 2 + side) * width
            dq_out[:, start:start + width] = dqrecv[col, side]
    for dx in REMOTE:
        remote(fsend.at[0], frecv.at[turn(dx)], fs.at[0], fr.at[turn(dx)], partner).wait_recv()
    for col in range(CHIPS):
        cols = slice(col * hw, (col + 1) * hw)
        dk_out[:, cols] = frecv[col, 0]
        dv_out[:, cols] = frecv[col, 1]

    q_copy(0, other).wait_send()
    do_copy(0, other).wait_send()
    rd_copy(0, other).wait_send()
    dq_copy(x, other).wait_send()
    for dx in REMOTE:
        k_copy(dx).wait_send()
        v_copy(dx).wait_send()
        f_copy(turn(dx)).wait_send()
        for side in range(2):
            q_copy(dx, side).wait_send()
            do_copy(dx, side).wait_send()
            rd_copy(dx, side).wait_send()
            dq_copy(turn(dx), side).wait_send()

    def sent_rows(r, c):
        k_row(r).wait_send()
        v_row(r).wait_send()
        return c

    def sent_on_chip(r, c):
        k_pass(r, core).wait_send()
        v_pass(r, core).wait_send()
        for kc in range(CHIPS):
            x_copy(r * CHIPS + kc).wait_send()
        return c

    def sent_terms(r, c):
        for kc in range(CHIPS):
            y_copy(r, kc).wait_send()
        return c

    lax.fori_loop(1, reach + 1, sent_rows, 0)
    lax.fori_loop(0, depth + 1, sent_on_chip, 0)
    lax.fori_loop(1, depth + 1, sent_terms, 0)


def on_device(seq_size, query, keys, values, output_gradient, forward_output, doc_ids):
    tok = query.shape[1]
    span = 2 * tok
    hw = HEAD_WIDTH
    width = PAIR * hw
    rows = seq_size // (2 * CHIPS)
    back = LONGEST // (CHIPS * span)
    slots = (back + 1) * CHIPS
    places = CHIPS * (back * CHIPS + 1)
    far = max(back, 1)
    bf, f32 = jnp.bfloat16, jnp.float32
    vmem = pl.BlockSpec(memory_space=pltpu.VMEM)
    dma = pltpu.SemaphoreType.DMA
    grad_query, grad_keys, grad_values = pl.pallas_call(
        functools.partial(kernel, rows, back),
        out_shape=(
            jax.ShapeDtypeStruct((tok, query.shape[2]), bf),
            jax.ShapeDtypeStruct((tok, keys.shape[2]), bf),
            jax.ShapeDtypeStruct((tok, keys.shape[2]), bf),
        ),
        in_specs=[vmem] * 6,
        out_specs=(vmem,) * 3,
        scratch_shapes=[
            pltpu.VMEM((CHIPS, tok + DOC_ROWS, hw), bf),
            pltpu.VMEM((2, slots, tok + DOC_ROWS, hw), bf),
            pltpu.VMEM((2, slots, tok, hw), bf),
            pltpu.VMEM((slots, span, 2 * hw), bf),
            pltpu.VMEM((slots, hw, span), bf),
            pltpu.VMEM((CHIPS, 2, 8, tok), f32),
            pltpu.VMEM((CHIPS, 2, tok, width), bf),
            pltpu.VMEM((CHIPS, 2, tok, width), bf),
            pltpu.VMEM((CHIPS, 2, 8, tok), f32),
            pltpu.VMEM((CHIPS, 2 * hw, PAIR * span), bf),
            pltpu.VMEM((CHIPS, PAIR * span, hw), bf),
            pltpu.VMEM((CHIPS, hw, PAIR * span), bf),
            pltpu.VMEM((CHIPS, PAIR * span, hw), bf),
            pltpu.VMEM((CHIPS, 1, PAIR * span), f32),
            pltpu.VMEM((places, span, PAIR * span), f32),
            pltpu.VMEM((places, 1, PAIR * span), f32),
            pltpu.VMEM((places, 1, PAIR * span), f32),
            pltpu.VMEM((places, 1, PAIR * span), f32),
            pltpu.VMEM((CHIPS, hw, PAIR * span), f32),
            pltpu.VMEM((slots, 2, 2, tok, hw), f32),
            pltpu.VMEM((slots, 2, tok, hw), f32),
            pltpu.VMEM((far, CHIPS, 2, tok, hw), bf),
            pltpu.VMEM((far, CHIPS, 2, tok, hw), bf),
            pltpu.VMEM((CHIPS, 2, tok, hw), bf),
            pltpu.VMEM((CHIPS, 2, tok, hw), bf),
            pltpu.VMEM((CHIPS, 2, tok, width), bf),
            pltpu.VMEM((CHIPS, 2, tok, width), bf),
            dma((CHIPS,)), dma((CHIPS,)), dma((CHIPS,)), dma((CHIPS,)),
            dma((CHIPS, 2)), dma((CHIPS, 2)), dma((CHIPS, 2)), dma((CHIPS, 2)),
            dma((CHIPS, 2)), dma((CHIPS, 2)),
            dma((back + 1,)), dma((back + 1,)), dma((back + 1,)), dma((back + 1,)),
            dma((back + 1,)), dma((back + 1,)), dma((back + 1,)), dma((back + 1,)),
            dma((slots,)), dma((slots,)), dma((far, CHIPS)), dma((far, CHIPS)),
            dma((CHIPS,)), dma((CHIPS,)), dma((CHIPS, 2)), dma((CHIPS, 2)),
        ],
        compiler_params=pltpu.CompilerParams(
            collective_id=0, has_side_effects=True, vmem_limit_bytes=56 * 1024 * 1024,
        ),
    )(query[0], keys[0], values[0], output_gradient[0], forward_output[0], doc_ids)
    return grad_query[None], grad_keys[None], grad_values[None]


def solution(mesh):
    wide = P("dp", "seq", None)
    return jax.shard_map(
        functools.partial(on_device, mesh.shape["seq"]),
        mesh=mesh,
        in_specs=(wide, wide, wide, wide, wide, P("dp", "seq")),
        out_specs=(wide, wide, wide),
        check_vma=False,
    )
```

time: 402 us -> 68.1 us (0.17)
  the two profiles are of different devices: /device:TPU:79 before, /device:TPU:23 now
where the time goes in v2:
time: 68.1 us; the launch traced here: 67.9 us
  Pallas kernels  63.7 us (94%)
  local copies, waits for them, and re-layouts  3.53 us (5%)
    pallas_call x1, Pallas kernels, on_device(): pl.pallas_call(functools.partial(kernel, rows, back), out_shape=(jax.Shap...  63.7 us
    unnamed x7, local copies, waits for them, and re-layouts  3.53 us

profile of v2, /device:TPU:23, one launch (start us, length us, event | category | flops | bytes accessed | tf_op | source)
XLA Modules:
  0.0 67.9 jit_solution(715115859386622644)
XLA Ops:
  0.6 63.7 %shard_map.85 = (bf16[128,2048]{1,0:T(8,128)(2,1)}, bf16[128,512]{1,0:T(8,128)(2,1)}, bf16[128,512]{1,0:T(8,128)(2,1)}) custom-call(bf16[128,2048]{1,0:T(8,128)(2,1)} %bitcast.9, bf16[128,512]{1,0:T(8,128)(2,1)} %bitcast.14, bf16[128,512]{1,0:T(8,128)(2,1)} %bitcast.15, bf16[128,2048]{1,0:T(8,128)(2,1)} %bitcast.10, bf16[128,2048]{1,0:T(8,128)(2,1)} %bitcast.11, ...), custom_call_target="tpu_custom_call" | custom-call | tf_op jit(solution)/shard_map/pallas_call | solution.py:498
  64.4 0.0 copy-start.1
  64.4 1.9 %copy.12 = bf16[1,128,2048]{2,1,0:T(8,128)(2,1)} copy(bf16[1,128,2048]{2,1,0:T(8,128)(2,1)} %bitcast.8) | data formatting | bytes 1048576
  66.3 0.0 copy-done.1
  66.3 0.0 copy-start
  66.3 0.7 copy.13
  67.0 0.3 copy-done
  67.3 0.7 copy.14
Async XLA Ops:
  64.4 1.9 %copy-start.1 = (bf16[128,512]{1,0:T(8,128)(2,1)S(1)}, bf16[128,512]{1,0:T(8,128)(2,1)}, u32[]{:S(2)}) copy-start(bf16[128,512]{1,0:T(8,128)(2,1)} %get-tuple-element.7) | copy-start | bytes 393220
  66.3 1.0 %copy-start = (bf16[128,512]{1,0:T(8,128)(2,1)S(1)}, bf16[128,512]{1,0:T(8,128)(2,1)}, u32[]{:S(2)}) copy-start(bf16[128,512]{1,0:T(8,128)(2,1)} %get-tuple-element.8) | copy-start | bytes 393220

commit v3 on v2

v3 whole, which is shorter than its diff:
```python
import functools
import math

import jax
import jax.numpy as jnp
from jax import lax
from jax.experimental import pallas as pl
from jax.experimental.pallas import tpu as pltpu
from jax.sharding import PartitionSpec as P

HEAD_WIDTH = 128
LONGEST = 2048
DOC_ROWS = 16
MASKED_LOW = -1e30
SCALE = 1.0 / math.sqrt(HEAD_WIDTH)
LOG2_SCALE = SCALE * math.log2(math.e)
CHIPS = 4
PAIR = 2


def nn(a, b):
    return jnp.dot(a, b, preferred_element_type=jnp.float32)


def kernel(
    rows, back,
    q_ref, k_ref, v_ref, do_ref, o_ref, id_ref,
    dq_out, dk_out, dv_out,
    ksend, kbuf, vbuf, k_x, k_t,
    rdsend, qbuf, dobuf, rdbuf, q_x, q_h, do_t, do_h, rd_h,
    e_all, m_all, p_low, s_low, dq_t,
    kv_acc, xrecv, ysend, yrecv, fsend, frecv, dqsend, dqrecv,
    ks, kr, vs, vr, qs, qr, gs, gr, rs, rr,
    kps, kpr, vps, vpr, kys, kyr, vys, vyr,
    xs, xr, ys, yr, fs, fr, ds, dr,
):
    tok = q_ref.shape[0]
    span = 2 * tok
    width = PAIR * HEAD_WIDTH
    hw = HEAD_WIDTH
    steps = back * CHIPS // 2 + 1
    me = lax.axis_index("seq")
    core = me % 2
    other = 1 - core
    x = (me // 2) % CHIPS
    y = me // (2 * CHIPS)
    mate = x + 1 - 2 * (x % 2)
    near, far = (mate + 2) % CHIPS, (x + 2) % CHIPS
    depth = jnp.minimum(y, back)
    reach = jnp.minimum(rows - 1 - y, back)

    def at(row, col, side):
        return {"seq": (row * CHIPS + col) * 2 + side}

    partner = at(y, x, other)

    barrier = pltpu.get_barrier_semaphore()
    pl.semaphore_signal(barrier, inc=1, device_id=partner)
    for col in (mate, near, far):
        for side in range(2):
            pl.semaphore_signal(barrier, inc=1, device_id=at(y, col, side))

    def greet_back(r, c):
        pl.semaphore_signal(barrier, inc=1, device_id=at(y - r, x, core))
        return c

    def greet_fwd(r, c):
        pl.semaphore_signal(barrier, inc=1, device_id=at(y + r, x, core))
        return c

    lax.fori_loop(1, depth + 1, greet_back, 0)
    lax.fori_loop(1, reach + 1, greet_fwd, 0)

    def feats(head, count):
        return pl.ds(pl.multiple_of(head * hw, hw), count * hw)

    def pair_cols(col, side):
        return feats(col * 2 * PAIR + side * PAIR, PAIR)

    doc_rows = lax.broadcasted_iota(jnp.int32, (DOC_ROWS, tok), 0)
    barred = jnp.where(doc_rows == id_ref[...], 0.0, MASKED_LOW).astype(jnp.bfloat16)
    for col in range(CHIPS):
        ksend[col, :tok, :] = k_ref[:, col * hw:(col + 1) * hw]
        ksend[col, tok:, :] = barred
    kbuf[core, x] = ksend[x]
    vbuf[core, x] = v_ref[:, feats(x, 1)]
    qbuf[x, core] = q_ref[:, pair_cols(x, core)]
    dobuf[x, core] = do_ref[:, pair_cols(x, core)]

    pl.semaphore_wait(barrier, 2 * CHIPS - 1 + depth + reach)

    def remote(src, dst, send, recv, target):
        return pltpu.make_async_remote_copy(
            src_ref=src, dst_ref=dst, send_sem=send, recv_sem=recv, device_id=target)

    def k_copy(col):
        return remote(ksend.at[col], kbuf.at[core, x], ks.at[col], kr.at[x], at(y, col, core))

    def v_copy(col):
        return remote(v_ref.at[:, feats(col, 1)], vbuf.at[core, x], vs.at[col], vr.at[x],
                      at(y, col, core))

    def q_copy(col, side):
        return remote(q_ref.at[:, pair_cols(col, side)], qbuf.at[x, core],
                      qs.at[col, side], qr.at[x, core], at(y, col, side))

    def do_copy(col, side):
        return remote(do_ref.at[:, pair_cols(col, side)], dobuf.at[x, core],
                      gs.at[col, side], gr.at[x, core], at(y, col, side))

    def rd_copy(col, side):
        return remote(rdsend.at[col, side], rdbuf.at[x, core],
                      rs.at[col, side], rr.at[x, core], at(y, col, side))

    def k_from(col):
        return remote(ksend.at[0], kbuf.at[core, col], ks.at[0], kr.at[col], partner)

    def v_from(col):
        return remote(v_ref.at[:, :hw], vbuf.at[core, col], vs.at[0], vr.at[col], partner)

    def q_from(col, side):
        return remote(q_ref.at[:, :width], qbuf.at[col, side], qs.at[0, 0], qr.at[col, side],
                      partner)

    def do_from(col, side):
        return remote(do_ref.at[:, :width], dobuf.at[col, side], gs.at[0, 0], gr.at[col, side],
                      partner)

    def rd_from(col, side):
        return remote(rdsend.at[0, 0], rdbuf.at[col, side], rs.at[0, 0], rr.at[col, side], partner)

    def row_of(r):
        return pl.ds(r * CHIPS, CHIPS)

    def k_pass(r, side):
        return remote(kbuf.at[side, row_of(r)], kbuf.at[side, row_of(r)], kps.at[r], kpr.at[r],
                      partner)

    def v_pass(r, side):
        return remote(vbuf.at[side, row_of(r)], vbuf.at[side, row_of(r)], vps.at[r], vpr.at[r],
                      partner)

    def k_row(r, target):
        return remote(kbuf.at[core, row_of(0)], kbuf.at[core, row_of(r)], kys.at[r], kyr.at[r],
                      target)

    def v_row(r, target):
        return remote(vbuf.at[core, row_of(0)], vbuf.at[core, row_of(r)], vys.at[r], vyr.at[r],
                      target)

    for col in (mate, far, near):
        k_copy(col).start()
    q_copy(x, other).start()
    for col in (mate, near):
        for side in range(2):
            q_copy(col, side).start()
    for col in (mate, far, near):
        v_copy(col).start()
    do_copy(x, other).start()
    for col in (mate, near):
        for side in range(2):
            do_copy(col, side).start()

    for col in range(CHIPS):
        for side in range(2):
            for g in range(PAIR):
                h = (col * 2 + side) * PAIR + g
                cols = slice(h * hw, (h + 1) * hw)
                prod = do_ref[:, cols].astype(jnp.float32) * o_ref[:, cols].astype(jnp.float32)
                rdsend[col, side, g:g + 1, :] = jnp.sum(
                    jnp.transpose(prod), axis=0, keepdims=True)
            rdsend[col, side, PAIR:, :] = jnp.zeros((8 - PAIR, tok), jnp.float32)
    rdbuf[x, core] = rdsend[x, core]
    rd_copy(x, other).start()
    for col in (mate, near, far):
        for side in range(2):
            rd_copy(col, side).start()
    kv_acc[...] = jnp.zeros(kv_acc.shape, jnp.float32)
    dq_t[...] = jnp.zeros(dq_t.shape, jnp.float32)

    def start_k_row(r, c):
        k_row(r, at(y + r, x, core)).start()
        return c

    def start_v_row(r, c):
        v_row(r, at(y + r, x, core)).start()
        return c

    def build_keys(r):
        def one(i, c):
            slot = r * CHIPS + i
            both = jnp.concatenate([kbuf[0, slot, :tok, :], kbuf[1, slot, :tok, :]], axis=0)
            bars = jnp.concatenate([kbuf[0, slot, tok:, :], kbuf[1, slot, tok:, :]], axis=1)
            pad = jnp.zeros((hw - DOC_ROWS, span), jnp.bfloat16)
            k_x[slot, :, :hw] = both
            k_x[slot, :, hw:] = jnp.transpose(jnp.concatenate([bars, pad], axis=0))
            k_t[slot] = jnp.transpose(both)
            return c

        lax.fori_loop(0, CHIPS, one, 0)

    for col in (mate, near, far):
        k_from(col).wait_recv()
    k_pass(0, core).start()
    lax.fori_loop(1, reach + 1, start_k_row, 0)
    k_pass(0, other).wait_recv()
    build_keys(0)

    tiles = [(c, g, slice((c * PAIR + g) * span, (c * PAIR + g + 1) * span))
             for c in range(2) for g in range(PAIR)]

    def x_copy(slot):
        return remote(kv_acc.at[slot, other], xrecv.at[slot], xs.at[slot], xr.at[slot], partner)

    def y_copy(r, kc):
        return remote(ysend.at[r - 1, kc], yrecv.at[r - 1, kc], ys.at[r - 1, kc],
                      yr.at[r - 1, kc], at(y - r, x, core))

    def dq_copy(col, side):
        return remote(dqsend.at[col, side], dqrecv.at[x, core], ds.at[col, side],
                      dr.at[x, core], at(y, col, side))

    def slot_of(block, u):
        chip = 2 * block + 1 - u
        return (y - chip // CHIPS) * CHIPS + chip % CHIPS

    def settle(block):
        for u in range(2):
            slot = slot_of(block, u)
            r, kc = slot // CHIPS, slot % CHIPS
            x_copy(slot).wait_recv()
            kv_sum = kv_acc[slot, core] + xrecv[slot]

            @pl.when(r > 0)
            def _():
                ysend[r - 1, kc] = kv_sum.astype(jnp.bfloat16)
                y_copy(r, kc).start()

            @pl.when(r == 0)
            def _():
                xrecv[slot] = kv_sum

    def pair_of_chunks(p, carry):
        a = (x // 2 + p) % 2
        b = 1 - a
        top = 2 * y + a
        count = jnp.minimum(top + 1, steps)

        for c in range(2):
            qc = 2 * a + c
            for side in range(2):
                @pl.when((qc != x) | (core != side))
                def _():
                    q_from(qc, side).wait_recv()
        for c, g, cols in tiles:
            qc = 2 * a + c
            head = slice(g * hw, (g + 1) * hw)
            both = jnp.concatenate([qbuf[qc, 0, :, head], qbuf[qc, 1, :, head]], axis=0)
            q_h[a, cols, :] = both
            q_x[a, :hw, cols] = jnp.transpose(both)
            bars = jnp.concatenate([kbuf[0, qc, tok:, :], kbuf[1, qc, tok:, :]], axis=1)
            q_x[a, hw:hw + DOC_ROWS, cols] = jnp.where(
                bars.astype(jnp.float32) == 0.0, 1.0, 0.0).astype(jnp.bfloat16)
        q_x[a, hw + DOC_ROWS:, :] = jnp.zeros((hw - DOC_ROWS, 2 * PAIR * span), jnp.bfloat16)

        def powers(t, stats, causal):
            out = []
            for (c, g, cols), (m_run, l_run) in zip(tiles, stats):
                for u in range(2):
                    s = nn(k_x[slot_of(top - t, u)], q_x[a, :, cols])
                    if causal and 1 - u == c:
                        key_pos = lax.broadcasted_iota(jnp.int32, (span, span), 0)
                        query_pos = lax.broadcasted_iota(jnp.int32, (span, span), 1)
                        s = jnp.where(key_pos <= query_pos, s, MASKED_LOW)
                    elif causal and 1 - u > c:
                        s = jnp.full((span, span), MASKED_LOW, jnp.float32)
                    m = jnp.max(s, axis=0, keepdims=True)
                    e = jnp.exp2((s - m) * LOG2_SCALE)
                    e_all[2 * t + u, :, cols] = e
                    m_all[2 * t + u, :, cols] = m
                    l = jnp.sum(e, axis=0, keepdims=True)
                    m_new = jnp.maximum(m_run, m)
                    l_run = (l_run * jnp.exp2((m_run - m_new) * LOG2_SCALE)
                             + l * jnp.exp2((m - m_new) * LOG2_SCALE))
                    m_run = m_new
                out.append((m_run, l_run))
            return tuple(out)

        def later_powers(t, stats):
            block = top - t
            r = y - block // 2

            @pl.when((p == 0) & (r > 0) & (block % 2 == 1))
            def _():
                k_row(r, partner).wait_recv()
                k_pass(r, core).start()
                k_pass(r, other).wait_recv()
                build_keys(r)

            return powers(t, stats, False)

        start = tuple((jnp.full((1, span), MASKED_LOW, jnp.float32),
                       jnp.zeros((1, span), jnp.float32)) for _ in tiles)
        stats = powers(0, start, True)

        @pl.when(p == 0)
        def _():
            for col in (mate, near, far):
                v_from(col).wait_recv()
            v_pass(0, core).start()
            lax.fori_loop(1, reach + 1, start_v_row, 0)

        stats = lax.fori_loop(1, count, later_powers, stats)
        m_top = jnp.concatenate([m for m, _ in stats], axis=1)
        inverse = 1.0 / jnp.concatenate([l for _, l in stats], axis=1)

        for c in range(2):
            qc = 2 * a + c
            for side in range(2):
                @pl.when((qc != x) | (core != side))
                def _():
                    do_from(qc, side).wait_recv()
                    rd_from(qc, side).wait_recv()

        @pl.when(p == 0)
        def _():
            for side in range(2):
                q_copy(far, side).start()
            for side in range(2):
                do_copy(far, side).start()
            v_pass(0, other).wait_recv()

        for c, g, cols in tiles:
            qc = 2 * a + c
            head = slice(g * hw, (g + 1) * hw)
            both = jnp.concatenate([dobuf[qc, 0, :, head], dobuf[qc, 1, :, head]], axis=0)
            do_h[a, cols, :] = both
            do_t[a, :, cols] = jnp.transpose(both)
            rd_h[a, :, cols] = jnp.concatenate(
                [rdbuf[qc, 0, g:g + 1, :], rdbuf[qc, 1, g:g + 1, :]], axis=1)

        def is_last(block):
            return (p == 1) | (block > 2 * y + b) | (block < 2 * y + b - steps + 1)

        def index(n):
            return jnp.where(p == 0, n, count - 1 - n)

        def terms(n, c):
            t = index(n)
            block = top - t
            r = y - block // 2

            @pl.when((p == 0) & (r > 0) & ((block % 2 == 1) | (n == 0)))
            def _():
                v_row(r, partner).wait_recv()
                v_pass(r, core).start()
                v_pass(r, other).wait_recv()

            for u in range(2):
                slot = slot_of(block, u)
                v_both = jnp.concatenate([vbuf[0, slot], vbuf[1, slot]], axis=0)
                ratio = jnp.exp2((m_all[2 * t + u] - m_top) * LOG2_SCALE) * inverse
                for _, _, cols in tiles:
                    dp = nn(v_both, do_t[a, :, cols])
                    pr = e_all[2 * t + u, :, cols] * ratio[:, cols]
                    p_low[u, :, cols] = pr.astype(jnp.bfloat16)
                    s_low[u, :, cols] = (pr * (dp - rd_h[a, :, cols])).astype(jnp.bfloat16)
                dv = nn(p_low[u], do_h[a])
                dk = nn(s_low[u], q_h[a]) * SCALE
                for side in range(2):
                    kv_acc[slot, side, 0] += dk[side * tok:(side + 1) * tok]
                    kv_acc[slot, side, 1] += dv[side * tok:(side + 1) * tok]
            dq_t[a] += nn(k_t[slot_of(block, 0)], s_low[0]) + nn(k_t[slot_of(block, 1)], s_low[1])

            @pl.when(is_last(block))
            def _():
                for u in range(2):
                    x_copy(slot_of(block, u)).start()

            @pl.when((n > 0) & is_last(top - index(n - 1)))
            def _():
                settle(top - index(n - 1))

            return c

        lax.fori_loop(0, count, terms, 0)

        @pl.when(is_last(top - index(count - 1)))
        def _():
            settle(top - index(count - 1))

        for c, g, cols in tiles:
            qc = 2 * a + c
            piece = jnp.transpose(dq_t[a, :, cols] * SCALE).astype(jnp.bfloat16)
            head = slice(g * hw, (g + 1) * hw)
            dqsend[qc, 0, :, head] = piece[:tok]
            dqsend[qc, 1, :, head] = piece[tok:]
        for c in range(2):
            qc = 2 * a + c
            for side in range(2):
                @pl.when((qc != x) | (core != side))
                def _():
                    dq_copy(qc, side).start()

        return carry

    lax.fori_loop(0, 2, pair_of_chunks, 0)

    def f_copy(col):
        return remote(fsend.at[col], frecv.at[x], fs.at[col], fr.at[x], at(y, col, core))

    def deliver(kc, c):
        def more(r, t):
            remote(ysend.at[0, 0], yrecv.at[r - 1, kc], ys.at[0, 0], yr.at[r - 1, kc],
                   partner).wait_recv()
            return t + yrecv[r - 1, kc].astype(jnp.float32)

        fsend[kc] = lax.fori_loop(1, reach + 1, more, xrecv[kc]).astype(jnp.bfloat16)

        @pl.when(kc != x)
        def _():
            f_copy(kc).start()

        return c

    lax.fori_loop(0, CHIPS, deliver, 0)

    frecv[x] = fsend[x]
    dqrecv[x, core] = dqsend[x, core]

    def dq_from(col, side):
        return remote(dqsend.at[0, 0], dqrecv.at[col, side], ds.at[0, 0], dr.at[col, side], partner)

    dq_from(x, other).wait_recv()
    for col in (mate, near, far):
        for side in range(2):
            dq_from(col, side).wait_recv()
    for col in range(CHIPS):
        for side in range(2):
            start = (col * 2 + side) * width
            dq_out[:, start:start + width] = dqrecv[col, side]
    for col in (mate, near, far):
        remote(fsend.at[0], frecv.at[col], fs.at[0], fr.at[col], partner).wait_recv()
    for col in range(CHIPS):
        cols = slice(col * hw, (col + 1) * hw)
        dk_out[:, cols] = frecv[col, 0]
        dv_out[:, cols] = frecv[col, 1]

    q_copy(x, other).wait_send()
    do_copy(x, other).wait_send()
    rd_copy(x, other).wait_send()
    dq_copy(x, other).wait_send()
    for col in (mate, near, far):
        k_copy(col).wait_send()
        v_copy(col).wait_send()
        f_copy(col).wait_send()
        for side in range(2):
            q_copy(col, side).wait_send()
            do_copy(col, side).wait_send()
            rd_copy(col, side).wait_send()
            dq_copy(col, side).wait_send()

    def sent_rows(r, c):
        k_row(r, partner).wait_send()
        v_row(r, partner).wait_send()
        return c

    def sent_on_chip(r, c):
        k_pass(r, core).wait_send()
        v_pass(r, core).wait_send()
        for kc in range(CHIPS):
            x_copy(r * CHIPS + kc).wait_send()
        return c

    def sent_terms(r, c):
        for kc in range(CHIPS):
            y_copy(r, kc).wait_send()
        return c

    lax.fori_loop(1, reach + 1, sent_rows, 0)
    lax.fori_loop(0, depth + 1, sent_on_chip, 0)
    lax.fori_loop(1, depth + 1, sent_terms, 0)


def on_device(seq_size, query, keys, values, output_gradient, forward_output, doc_ids):
    tok = query.shape[1]
    span = 2 * tok
    hw = HEAD_WIDTH
    width = PAIR * hw
    rows = seq_size // (2 * CHIPS)
    back = LONGEST // (CHIPS * span)
    slots = (back + 1) * CHIPS
    places = back * CHIPS + 2
    wide = 2 * PAIR * span
    far = max(back, 1)
    bf, f32 = jnp.bfloat16, jnp.float32
    vmem = pl.BlockSpec(memory_space=pltpu.VMEM)
    dma = pltpu.SemaphoreType.DMA
    grad_query, grad_keys, grad_values = pl.pallas_call(
        functools.partial(kernel, rows, back),
        out_shape=(
            jax.ShapeDtypeStruct((tok, query.shape[2]), bf),
            jax.ShapeDtypeStruct((tok, keys.shape[2]), bf),
            jax.ShapeDtypeStruct((tok, keys.shape[2]), bf),
        ),
        in_specs=[vmem] * 6,
        out_specs=(vmem,) * 3,
        scratch_shapes=[
            pltpu.VMEM((CHIPS, tok + DOC_ROWS, hw), bf),
            pltpu.VMEM((2, slots, tok + DOC_ROWS, hw), bf),
            pltpu.VMEM((2, slots, tok, hw), bf),
            pltpu.VMEM((slots, span, 2 * hw), bf),
            pltpu.VMEM((slots, hw, span), bf),
            pltpu.VMEM((CHIPS, 2, 8, tok), f32),
            pltpu.VMEM((CHIPS, 2, tok, width), bf),
            pltpu.VMEM((CHIPS, 2, tok, width), bf),
            pltpu.VMEM((CHIPS, 2, 8, tok), f32),
            pltpu.VMEM((2, 2 * hw, wide), bf),
            pltpu.VMEM((2, wide, hw), bf),
            pltpu.VMEM((2, hw, wide), bf),
            pltpu.VMEM((2, wide, hw), bf),
            pltpu.VMEM((2, 1, wide), f32),
            pltpu.VMEM((places, span, wide), f32),
            pltpu.VMEM((places, 1, wide), f32),
            pltpu.VMEM((2, span, wide), bf),
            pltpu.VMEM((2, span, wide), bf),
            pltpu.VMEM((2, hw, wide), f32),
            pltpu.VMEM((slots, 2, 2, tok, hw), f32),
            pltpu.VMEM((slots, 2, tok, hw), f32),
            pltpu.VMEM((far, CHIPS, 2, tok, hw), bf),
            pltpu.VMEM((far, CHIPS, 2, tok, hw), bf),
            pltpu.VMEM((CHIPS, 2, tok, hw), bf),
            pltpu.VMEM((CHIPS, 2, tok, hw), bf),
            pltpu.VMEM((CHIPS, 2, tok, width), bf),
            pltpu.VMEM((CHIPS, 2, tok, width), bf),
            dma((CHIPS,)), dma((CHIPS,)), dma((CHIPS,)), dma((CHIPS,)),
            dma((CHIPS, 2)), dma((CHIPS, 2)), dma((CHIPS, 2)), dma((CHIPS, 2)),
            dma((CHIPS, 2)), dma((CHIPS, 2)),
            dma((back + 1,)), dma((back + 1,)), dma((back + 1,)), dma((back + 1,)),
            dma((back + 1,)), dma((back + 1,)), dma((back + 1,)), dma((back + 1,)),
            dma((slots,)), dma((slots,)), dma((far, CHIPS)), dma((far, CHIPS)),
            dma((CHIPS,)), dma((CHIPS,)), dma((CHIPS, 2)), dma((CHIPS, 2)),
        ],
        compiler_params=pltpu.CompilerParams(
            collective_id=0, has_side_effects=True, vmem_limit_bytes=56 * 1024 * 1024,
        ),
    )(query[0], keys[0], values[0], output_gradient[0], forward_output[0], doc_ids)
    return grad_query[None], grad_keys[None], grad_values[None]


def solution(mesh):
    wide = P("dp", "seq", None)
    return jax.shard_map(
        functools.partial(on_device, mesh.shape["seq"]),
        mesh=mesh,
        in_specs=(wide, wide, wide, wide, wide, P("dp", "seq")),
        out_specs=(wide, wide, wide),
        check_vma=False,
    )
```

time: 68.1 us -> 61.4 us (0.902)
  Pallas kernels: 63.7 us -> 57.1 us
    pallas_call x1, Pallas kernels: 63.7 us -> 57.1 us  [on_device(): pl.pallas_call(functools.partial(kernel, rows, back), out_shape=(jax.Shap...]
where the time goes in v3:
time: 61.4 us; the launch traced here: 61.2 us
  Pallas kernels  57.1 us (93%)
  local copies, waits for them, and re-layouts  3.53 us (6%)
  between operations  0.65 us (1%)
    pallas_call x1, Pallas kernels, on_device(): pl.pallas_call(functools.partial(kernel, rows, back), out_shape=(jax.Shap...  57.1 us
    unnamed x7, local copies, waits for them, and re-layouts  3.53 us

profile of v3, /device:TPU:23, one launch (start us, length us, event | category | flops | bytes accessed | tf_op | source)
XLA Modules:
  0.0 61.2 jit_solution(6410302431538453445)
XLA Ops:
  0.6 57.1 %shard_map.85 = (bf16[128,2048]{1,0:T(8,128)(2,1)}, bf16[128,512]{1,0:T(8,128)(2,1)}, bf16[128,512]{1,0:T(8,128)(2,1)}) custom-call(bf16[128,2048]{1,0:T(8,128)(2,1)} %bitcast.9, bf16[128,512]{1,0:T(8,128)(2,1)} %bitcast.14, bf16[128,512]{1,0:T(8,128)(2,1)} %bitcast.15, bf16[128,2048]{1,0:T(8,128)(2,1)} %bitcast.10, bf16[128,2048]{1,0:T(8,128)(2,1)} %bitcast.11, ...), custom_call_target="tpu_custom_call" | custom-call | tf_op jit(solution)/shard_map/pallas_call | solution.py:499
  57.7 0.0 copy-start.1
  57.7 1.9 %copy.12 = bf16[1,128,2048]{2,1,0:T(8,128)(2,1)} copy(bf16[1,128,2048]{2,1,0:T(8,128)(2,1)} %bitcast.8) | data formatting | bytes 1048576
  59.6 0.0 copy-done.1
  59.6 0.0 copy-start
  59.6 0.7 %copy.13 = bf16[1,128,512]{2,1,0:T(8,128)(2,1)} copy(bf16[1,128,512]{2,1,0:T(8,128)(2,1)S(1)} %bitcast.13) | data formatting | bytes 262144
  60.3 0.3 copy-done
  60.6 0.7 %copy.14 = bf16[1,128,512]{2,1,0:T(8,128)(2,1)} copy(bf16[1,128,512]{2,1,0:T(8,128)(2,1)S(1)} %bitcast.12) | data formatting | bytes 262144
Async XLA Ops:
  57.7 1.9 %copy-start.1 = (bf16[128,512]{1,0:T(8,128)(2,1)S(1)}, bf16[128,512]{1,0:T(8,128)(2,1)}, u32[]{:S(2)}) copy-start(bf16[128,512]{1,0:T(8,128)(2,1)} %get-tuple-element.7) | copy-start | bytes 393220
  59.6 1.0 %copy-start = (bf16[128,512]{1,0:T(8,128)(2,1)S(1)}, bf16[128,512]{1,0:T(8,128)(2,1)}, u32[]{:S(2)}) copy-start(bf16[128,512]{1,0:T(8,128)(2,1)} %get-tuple-element.8) | copy-start | bytes 393220

commit v4 on v3

v4 whole, which is shorter than its diff:
```python
import functools
import math

import jax
import jax.numpy as jnp
from jax import lax
from jax.experimental import pallas as pl
from jax.experimental.pallas import tpu as pltpu
from jax.sharding import PartitionSpec as P

HEAD_WIDTH = 128
LONGEST = 2048
DOC_ROWS = 16
MASKED_LOW = -1e30
SCALE = 1.0 / math.sqrt(HEAD_WIDTH)
LOG2_SCALE = SCALE * math.log2(math.e)
CHIPS = 4
PAIR = 2


def nn(a, b):
    return jnp.dot(a, b, preferred_element_type=jnp.float32)


def kernel(
    rows, back,
    q_ref, k_ref, v_ref, do_ref, o_ref, id_ref,
    dqrecv, frecv,
    ksend, kbuf, vbuf, k_x, k_t,
    rdsend, qbuf, dobuf, rdbuf, q_x, q_h, do_t, do_h, rd_h,
    e_all, m_all, top_all, inv_all, p_low, s_low, dq_t,
    kv_acc, xrecv, ysend, yrecv, fsend, dqsend,
    ks, kr, vs, vr, qs, qr, gs, gr, rs, rr,
    kps, kpr, vps, vpr, kys, kyr, vys, vyr,
    xs, xr, ys, yr, fs, fr, ds, dr,
):
    tok = q_ref.shape[0]
    span = 2 * tok
    width = PAIR * HEAD_WIDTH
    hw = HEAD_WIDTH
    steps = back * CHIPS // 2 + 1
    me = lax.axis_index("seq")
    core = me % 2
    other = 1 - core
    x = (me // 2) % CHIPS
    y = me // (2 * CHIPS)
    mate = x + 1 - 2 * (x % 2)
    near, far = (mate + 2) % CHIPS, (x + 2) % CHIPS
    depth = jnp.minimum(y, back)
    reach = jnp.minimum(rows - 1 - y, back)

    def at(row, col, side):
        return {"seq": (row * CHIPS + col) * 2 + side}

    partner = at(y, x, other)

    barrier = pltpu.get_barrier_semaphore()
    pl.semaphore_signal(barrier, inc=1, device_id=partner)
    for col in (mate, near, far):
        for side in range(2):
            pl.semaphore_signal(barrier, inc=1, device_id=at(y, col, side))

    def greet_back(r, c):
        pl.semaphore_signal(barrier, inc=1, device_id=at(y - r, x, core))
        return c

    def greet_fwd(r, c):
        pl.semaphore_signal(barrier, inc=1, device_id=at(y + r, x, core))
        return c

    lax.fori_loop(1, depth + 1, greet_back, 0)
    lax.fori_loop(1, reach + 1, greet_fwd, 0)

    def feats(head, count):
        return pl.ds(pl.multiple_of(head * hw, hw), count * hw)

    def pair_cols(col, side):
        return feats(col * 2 * PAIR + side * PAIR, PAIR)

    doc_rows = lax.broadcasted_iota(jnp.int32, (DOC_ROWS, tok), 0)
    barred = jnp.where(doc_rows == id_ref[...], 0.0, MASKED_LOW).astype(jnp.bfloat16)
    for col in range(CHIPS):
        ksend[col, :tok, :] = k_ref[:, col * hw:(col + 1) * hw]
        ksend[col, tok:, :] = barred
    kbuf[core, x] = ksend[x]
    vbuf[core, x] = v_ref[:, feats(x, 1)]
    qbuf[x, core] = q_ref[:, pair_cols(x, core)]
    dobuf[x, core] = do_ref[:, pair_cols(x, core)]

    pl.semaphore_wait(barrier, 2 * CHIPS - 1 + depth + reach)

    def remote(src, dst, send, recv, target):
        return pltpu.make_async_remote_copy(
            src_ref=src, dst_ref=dst, send_sem=send, recv_sem=recv, device_id=target)

    def k_copy(col):
        return remote(ksend.at[col], kbuf.at[core, x], ks.at[col], kr.at[x], at(y, col, core))

    def v_copy(col):
        return remote(v_ref.at[:, feats(col, 1)], vbuf.at[core, x], vs.at[col], vr.at[x],
                      at(y, col, core))

    def q_copy(col, side):
        return remote(q_ref.at[:, pair_cols(col, side)], qbuf.at[x, core],
                      qs.at[col, side], qr.at[x, core], at(y, col, side))

    def do_copy(col, side):
        return remote(do_ref.at[:, pair_cols(col, side)], dobuf.at[x, core],
                      gs.at[col, side], gr.at[x, core], at(y, col, side))

    def rd_copy(col, side):
        return remote(rdsend.at[col, side], rdbuf.at[x, core],
                      rs.at[col, side], rr.at[x, core], at(y, col, side))

    def k_from(col):
        return remote(ksend.at[0], kbuf.at[core, col], ks.at[0], kr.at[col], partner)

    def v_from(col):
        return remote(v_ref.at[:, :hw], vbuf.at[core, col], vs.at[0], vr.at[col], partner)

    def q_from(col, side):
        return remote(q_ref.at[:, :width], qbuf.at[col, side], qs.at[0, 0], qr.at[col, side],
                      partner)

    def do_from(col, side):
        return remote(do_ref.at[:, :width], dobuf.at[col, side], gs.at[0, 0], gr.at[col, side],
                      partner)

    def rd_from(col, side):
        return remote(rdsend.at[0, 0], rdbuf.at[col, side], rs.at[0, 0], rr.at[col, side], partner)

    def row_of(r):
        return pl.ds(r * CHIPS, CHIPS)

    def k_pass(r, side):
        return remote(kbuf.at[side, row_of(r)], kbuf.at[side, row_of(r)], kps.at[r], kpr.at[r],
                      partner)

    def v_pass(r, side):
        return remote(vbuf.at[side, row_of(r)], vbuf.at[side, row_of(r)], vps.at[r], vpr.at[r],
                      partner)

    def k_row(r, target):
        return remote(kbuf.at[core, row_of(0)], kbuf.at[core, row_of(r)], kys.at[r], kyr.at[r],
                      target)

    def v_row(r, target):
        return remote(vbuf.at[core, row_of(0)], vbuf.at[core, row_of(r)], vys.at[r], vyr.at[r],
                      target)

    for col in (mate, far, near):
        k_copy(col).start()
    for col in (mate, far, near):
        v_copy(col).start()
    def start_k_row(r, c):
        k_row(r, at(y + r, x, core)).start()
        return c

    def start_v_row(r, c):
        v_row(r, at(y + r, x, core)).start()
        return c

    def build_keys(r):
        def one(i, c):
            slot = r * CHIPS + i
            both = jnp.concatenate([kbuf[0, slot, :tok, :], kbuf[1, slot, :tok, :]], axis=0)
            bars = jnp.concatenate([kbuf[0, slot, tok:, :], kbuf[1, slot, tok:, :]], axis=1)
            pad = jnp.zeros((hw - DOC_ROWS, span), jnp.bfloat16)
            k_x[slot, :, :hw] = both
            k_x[slot, :, hw:] = jnp.transpose(jnp.concatenate([bars, pad], axis=0))
            k_t[slot] = jnp.transpose(both)
            return c

        lax.fori_loop(0, CHIPS, one, 0)

    for col in (mate, near, far):
        k_from(col).wait_recv()
    k_pass(0, core).start()
    lax.fori_loop(1, reach + 1, start_k_row, 0)
    for col in (mate, near, far):
        v_from(col).wait_recv()
    v_pass(0, core).start()
    lax.fori_loop(1, reach + 1, start_v_row, 0)
    q_copy(x, other).start()
    for col in (mate, near, far):
        for side in range(2):
            q_copy(col, side).start()

    for col in range(CHIPS):
        for side in range(2):
            for g in range(PAIR):
                h = (col * 2 + side) * PAIR + g
                cols = slice(h * hw, (h + 1) * hw)
                prod = do_ref[:, cols].astype(jnp.float32) * o_ref[:, cols].astype(jnp.float32)
                rdsend[col, side, g:g + 1, :] = jnp.sum(
                    jnp.transpose(prod), axis=0, keepdims=True)
            rdsend[col, side, PAIR:, :] = jnp.zeros((8 - PAIR, tok), jnp.float32)
    rdbuf[x, core] = rdsend[x, core]
    rd_copy(x, other).start()
    for col in (mate, near, far):
        for side in range(2):
            rd_copy(col, side).start()
    kv_acc[...] = jnp.zeros(kv_acc.shape, jnp.float32)
    dq_t[...] = jnp.zeros(dq_t.shape, jnp.float32)

    k_pass(0, other).wait_recv()
    build_keys(0)

    def pass_k_row(r, c):
        k_row(r, partner).wait_recv()
        k_pass(r, core).start()
        return c

    def have_k_row(r, c):
        k_pass(r, other).wait_recv()
        build_keys(r)
        return c

    def pass_v_row(r, c):
        v_row(r, partner).wait_recv()
        v_pass(r, core).start()
        return c

    def have_v_row(r, c):
        v_pass(r, other).wait_recv()
        return c

    lax.fori_loop(1, depth + 1, pass_k_row, 0)
    lax.fori_loop(1, depth + 1, have_k_row, 0)

    tiles = [(c, g, slice((c * PAIR + g) * span, (c * PAIR + g + 1) * span))
             for c in range(2) for g in range(PAIR)]

    def place_of(block):
        return (y - block // 2) * 2 + block % 2

    def x_copy(place):
        return remote(kv_acc.at[place, other], xrecv.at[place], xs.at[place], xr.at[place], partner)

    def y_copy(r, part):
        return remote(ysend.at[r - 1, part], yrecv.at[r - 1, part], ys.at[r - 1, part],
                      yr.at[r - 1, part], at(y - r, x, core))

    def dq_copy(col, side):
        return remote(dqsend.at[col, side], dqrecv.at[x, core], ds.at[col, side],
                      dr.at[x, core], at(y, col, side))

    def settle(block):
        place = place_of(block)
        r, part = place // 2, place % 2
        x_copy(place).wait_recv()
        kv_sum = kv_acc[place, core] + xrecv[place]

        @pl.when(r > 0)
        def _():
            ysend[r - 1, part] = kv_sum.astype(jnp.bfloat16)
            y_copy(r, part).start()

        @pl.when(r == 0)
        def _():
            xrecv[place] = kv_sum

    def chunks_of(p):
        a = (x // 2 + p) % 2
        top = 2 * y + a
        return a, top, jnp.minimum(top + 1, steps)

    def first_pass(p, carry):
        a, top, count = chunks_of(p)

        @pl.when(p == 1)
        def _():
            lax.fori_loop(1, depth + 1, pass_v_row, 0)

        for c in range(2):
            qc = 2 * a + c
            for side in range(2):
                @pl.when((qc != x) | (core != side))
                def _():
                    q_from(qc, side).wait_recv()
        @pl.when(p == 0)
        def _():
            do_copy(x, other).start()
            for col in (mate, near, far):
                for side in range(2):
                    do_copy(col, side).start()

        for c, g, cols in tiles:
            qc = 2 * a + c
            head = slice(g * hw, (g + 1) * hw)
            both = jnp.concatenate([qbuf[qc, 0, :, head], qbuf[qc, 1, :, head]], axis=0)
            q_h[a, cols, :] = both
            q_x[a, :hw, cols] = jnp.transpose(both)
            bars = jnp.concatenate([kbuf[0, qc, tok:, :], kbuf[1, qc, tok:, :]], axis=1)
            q_x[a, hw:hw + DOC_ROWS, cols] = jnp.where(
                bars.astype(jnp.float32) == 0.0, 1.0, 0.0).astype(jnp.bfloat16)
        q_x[a, hw + DOC_ROWS:, :] = jnp.zeros((hw - DOC_ROWS, 2 * PAIR * span), jnp.bfloat16)

        def powers(t, stats, causal):
            place = place_of(top - t)
            keys_x = k_x[pl.ds(2 * place, 2)].reshape(2 * span, 2 * hw)
            out = []
            for (c, g, cols), (m_run, l_run) in zip(tiles, stats):
                s = nn(keys_x, q_x[a, :, cols])
                if causal:
                    key_pos = lax.broadcasted_iota(jnp.int32, (2 * span, span), 0)
                    query_pos = lax.broadcasted_iota(jnp.int32, (2 * span, span), 1)
                    s = jnp.where(key_pos <= query_pos + c * span, s, MASKED_LOW)
                m = jnp.max(s, axis=0, keepdims=True)
                e = jnp.exp2((s - m) * LOG2_SCALE)
                e_all[a, t, :, cols] = e
                m_all[a, t, :, cols] = m
                l = jnp.sum(e, axis=0, keepdims=True)
                m_new = jnp.maximum(m_run, m)
                l_run = (l_run * jnp.exp2((m_run - m_new) * LOG2_SCALE)
                         + l * jnp.exp2((m - m_new) * LOG2_SCALE))
                out.append((m_new, l_run))
            return tuple(out)

        def later_powers(t, stats):
            return powers(t, stats, False)

        start = tuple((jnp.full((1, span), MASKED_LOW, jnp.float32),
                       jnp.zeros((1, span), jnp.float32)) for _ in tiles)
        stats = powers(0, start, True)
        stats = lax.fori_loop(1, count, later_powers, stats)
        top_all[a] = jnp.concatenate([m for m, _ in stats], axis=1)
        inv_all[a] = 1.0 / jnp.concatenate([l for _, l in stats], axis=1)
        return carry

    lax.fori_loop(0, 2, first_pass, 0)
    def take_gradients(p, carry):
        a = (x // 2 + p) % 2
        for c in range(2):
            qc = 2 * a + c
            for side in range(2):
                @pl.when((qc != x) | (core != side))
                def _():
                    do_from(qc, side).wait_recv()
                    rd_from(qc, side).wait_recv()
        for c, g, cols in tiles:
            qc = 2 * a + c
            head = slice(g * hw, (g + 1) * hw)
            both = jnp.concatenate([dobuf[qc, 0, :, head], dobuf[qc, 1, :, head]], axis=0)
            do_h[a, cols, :] = both
            do_t[a, :, cols] = jnp.transpose(both)
            rd_h[a, :, cols] = jnp.concatenate(
                [rdbuf[qc, 0, g:g + 1, :], rdbuf[qc, 1, g:g + 1, :]], axis=1)
        return carry

    lax.fori_loop(0, 2, take_gradients, 0)
    lax.fori_loop(0, depth + 1, have_v_row, 0)

    own = x // 2
    away = 1 - own
    low = 2 * y - 2 * back
    lead = 1 + away
    shared = 4 * back - 1

    def item(n):
        i = n - lead
        j = i - 1
        in_lead, in_tail = n < lead, i >= shared
        block = jnp.where(
            in_lead, 2 * y + n,
            jnp.where(in_tail, 2 * y + i - shared,
                      jnp.where(i == 0, low, low + 1 + j // 2)))
        a = jnp.where(
            in_lead, away,
            jnp.where(in_tail, own, jnp.where(i == 0, 0, jnp.where(j % 2 == 0, away, own))))
        final = jnp.where(in_lead, n == 1, in_tail | (i % 2 == 0))
        return a, block, final & (block >= 0)

    def send_queries(a):
        for c, g, cols in tiles:
            qc = 2 * a + c
            piece = jnp.transpose(dq_t[a, :, cols] * SCALE).astype(jnp.bfloat16)
            head = slice(g * hw, (g + 1) * hw)
            dqsend[qc, 0, :, head] = piece[:tok]
            dqsend[qc, 1, :, head] = piece[tok:]
        for c in range(2):
            qc = 2 * a + c
            for side in range(2):
                @pl.when((qc != x) | (core != side))
                def _():
                    dq_copy(qc, side).start()

    def terms(n, c):
        a, block, final = item(n)

        @pl.when(block >= 0)
        def _():
            t = 2 * y + a - block
            place = place_of(block)
            v_both = jnp.concatenate(
                [vbuf[i, 2 * place + u] for u in range(2) for i in range(2)], axis=0)
            ratio = jnp.exp2((m_all[a, t] - top_all[a]) * LOG2_SCALE) * inv_all[a]
            for _, _, cols in tiles:
                dp = nn(v_both, do_t[a, :, cols])
                pr = e_all[a, t, :, cols] * ratio[:, cols]
                p_low[:, cols] = pr.astype(jnp.bfloat16)
                s_low[:, cols] = (pr * (dp - rd_h[a, :, cols])).astype(jnp.bfloat16)
            dv = nn(p_low[...], do_h[a])
            dk = nn(s_low[...], q_h[a]) * SCALE
            for u in range(2):
                for side in range(2):
                    piece = slice((2 * u + side) * tok, (2 * u + side + 1) * tok)
                    kv_acc[place, side, u, 0] += dk[piece]
                    kv_acc[place, side, u, 1] += dv[piece]
            dq_t[a] += nn(jnp.concatenate([k_t[2 * place], k_t[2 * place + 1]], axis=1), s_low[...])

        @pl.when(final)
        def _():
            x_copy(place_of(block)).start()

        before, final_before = item(n - 1)[1:]

        @pl.when((n > 0) & final_before)
        def _():
            settle(before)

        @pl.when(n == lead + shared - 2)
        def _():
            send_queries(away)

        return c

    last = lead + shared + own
    lax.fori_loop(0, last + 1, terms, 0)
    send_queries(own)
    settle(item(last)[1])

    def f_copy(col):
        return remote(fsend.at[col], frecv.at[x], fs.at[col], fr.at[x], at(y, col, core))

    def deliver(part, c):
        def more(r, t):
            remote(ysend.at[0, 0], yrecv.at[r - 1, part], ys.at[0, 0], yr.at[r - 1, part],
                   partner).wait_recv()
            return t + yrecv[r - 1, part].astype(jnp.float32)

        both = lax.fori_loop(1, reach + 1, more, xrecv[part]).astype(jnp.bfloat16)
        for u in range(2):
            kc = 2 * part + u
            fsend[kc] = both[u]

            @pl.when(kc != x)
            def _():
                f_copy(kc).start()

        return c

    lax.fori_loop(0, 2, deliver, 0)

    frecv[x] = fsend[x]
    dqrecv[x, core] = dqsend[x, core]

    def dq_from(col, side):
        return remote(dqsend.at[0, 0], dqrecv.at[col, side], ds.at[0, 0], dr.at[col, side], partner)

    dq_from(x, other).wait_recv()
    for col in (mate, near, far):
        for side in range(2):
            dq_from(col, side).wait_recv()
    for col in (mate, near, far):
        remote(fsend.at[0], frecv.at[col], fs.at[0], fr.at[col], partner).wait_recv()
    q_copy(x, other).wait_send()
    do_copy(x, other).wait_send()
    rd_copy(x, other).wait_send()
    dq_copy(x, other).wait_send()
    for col in (mate, near, far):
        k_copy(col).wait_send()
        v_copy(col).wait_send()
        f_copy(col).wait_send()
        for side in range(2):
            q_copy(col, side).wait_send()
            do_copy(col, side).wait_send()
            rd_copy(col, side).wait_send()
            dq_copy(col, side).wait_send()

    def sent_rows(r, c):
        k_row(r, partner).wait_send()
        v_row(r, partner).wait_send()
        return c

    def sent_on_chip(r, c):
        k_pass(r, core).wait_send()
        v_pass(r, core).wait_send()
        for part in range(2):
            x_copy(r * 2 + part).wait_send()
        return c

    def sent_terms(r, c):
        for part in range(2):
            y_copy(r, part).wait_send()
        return c

    lax.fori_loop(1, reach + 1, sent_rows, 0)
    lax.fori_loop(0, depth + 1, sent_on_chip, 0)
    lax.fori_loop(1, depth + 1, sent_terms, 0)


def lay_out(dq_raw, kv_raw, dq_out, dk_out, dv_out):
    width = dq_raw.shape[3]
    hw = kv_raw.shape[3]
    for col in range(CHIPS):
        for side in range(2):
            start = (col * 2 + side) * width
            dq_out[0, :, start:start + width] = dq_raw[col, side]
        cols = slice(col * hw, (col + 1) * hw)
        dk_out[0, :, cols] = kv_raw[col, 0]
        dv_out[0, :, cols] = kv_raw[col, 1]


def on_device(seq_size, query, keys, values, output_gradient, forward_output, doc_ids):
    tok = query.shape[1]
    span = 2 * tok
    hw = HEAD_WIDTH
    width = PAIR * hw
    rows = seq_size // (2 * CHIPS)
    back = LONGEST // (CHIPS * span)
    slots = (back + 1) * CHIPS
    wide = 2 * PAIR * span
    far = max(back, 1)
    bf, f32 = jnp.bfloat16, jnp.float32
    vmem = pl.BlockSpec(memory_space=pltpu.VMEM)
    dma = pltpu.SemaphoreType.DMA
    dq_raw, kv_raw = pl.pallas_call(
        functools.partial(kernel, rows, back),
        out_shape=(
            jax.ShapeDtypeStruct((CHIPS, 2, tok, width), bf),
            jax.ShapeDtypeStruct((CHIPS, 2, tok, hw), bf),
        ),
        in_specs=[vmem] * 6,
        out_specs=(vmem,) * 2,
        scratch_shapes=[
            pltpu.VMEM((CHIPS, tok + DOC_ROWS, hw), bf),
            pltpu.VMEM((2, slots, tok + DOC_ROWS, hw), bf),
            pltpu.VMEM((2, slots, tok, hw), bf),
            pltpu.VMEM((slots, span, 2 * hw), bf),
            pltpu.VMEM((slots, hw, span), bf),
            pltpu.VMEM((CHIPS, 2, 8, tok), f32),
            pltpu.VMEM((CHIPS, 2, tok, width), bf),
            pltpu.VMEM((CHIPS, 2, tok, width), bf),
            pltpu.VMEM((CHIPS, 2, 8, tok), f32),
            pltpu.VMEM((2, 2 * hw, wide), bf),
            pltpu.VMEM((2, wide, hw), bf),
            pltpu.VMEM((2, hw, wide), bf),
            pltpu.VMEM((2, wide, hw), bf),
            pltpu.VMEM((2, 1, wide), f32),
            pltpu.VMEM((2, back * 2 + 1, 2 * span, wide), f32),
            pltpu.VMEM((2, back * 2 + 1, 1, wide), f32),
            pltpu.VMEM((2, 1, wide), f32),
            pltpu.VMEM((2, 1, wide), f32),
            pltpu.VMEM((2 * span, wide), bf),
            pltpu.VMEM((2 * span, wide), bf),
            pltpu.VMEM((2, hw, wide), f32),
            pltpu.VMEM((slots // 2, 2, 2, 2, tok, hw), f32),
            pltpu.VMEM((slots // 2, 2, 2, tok, hw), f32),
            pltpu.VMEM((far, 2, 2, 2, tok, hw), bf),
            pltpu.VMEM((far, 2, 2, 2, tok, hw), bf),
            pltpu.VMEM((CHIPS, 2, tok, hw), bf),
            pltpu.VMEM((CHIPS, 2, tok, width), bf),
            dma((CHIPS,)), dma((CHIPS,)), dma((CHIPS,)), dma((CHIPS,)),
            dma((CHIPS, 2)), dma((CHIPS, 2)), dma((CHIPS, 2)), dma((CHIPS, 2)),
            dma((CHIPS, 2)), dma((CHIPS, 2)),
            dma((back + 1,)), dma((back + 1,)), dma((back + 1,)), dma((back + 1,)),
            dma((back + 1,)), dma((back + 1,)), dma((back + 1,)), dma((back + 1,)),
            dma((slots // 2,)), dma((slots // 2,)), dma((far, 2)), dma((far, 2)),
            dma((CHIPS,)), dma((CHIPS,)), dma((CHIPS, 2)), dma((CHIPS, 2)),
        ],
        compiler_params=pltpu.CompilerParams(
            collective_id=0, has_side_effects=True, vmem_limit_bytes=56 * 1024 * 1024,
        ),
    )(query[0], keys[0], values[0], output_gradient[0], forward_output[0], doc_ids)
    return pl.pallas_call(
        lay_out,
        out_shape=(
            jax.ShapeDtypeStruct(query.shape, bf),
            jax.ShapeDtypeStruct(keys.shape, bf),
            jax.ShapeDtypeStruct(keys.shape, bf),
        ),
        in_specs=[vmem] * 2,
        out_specs=(vmem,) * 3,
    )(dq_raw, kv_raw)


def solution(mesh):
    wide = P("dp", "seq", None)
    return jax.shard_map(
        functools.partial(on_device, mesh.shape["seq"]),
        mesh=mesh,
        in_specs=(wide, wide, wide, wide, wide, P("dp", "seq")),
        out_specs=(wide, wide, wide),
        check_vma=False,
    )
```

time: 61.4 us -> 56.8 us (0.925)
  the two profiles are of different devices: /device:TPU:23 before, /device:TPU:79 now
where the time goes in v4:
time: 56.8 us; the launch traced here: 56.7 us
  Pallas kernels  56 us (99%)
  between operations  0.64 us (1%)
    pallas_call x1, Pallas kernels, on_device(): pl.pallas_call(functools.partial(kernel, rows, back), out_shape=(jax.Shap...  54 us
    pallas_call x1, Pallas kernels, on_device(): pl.pallas_call(lay_out, out_shape=(jax.ShapeDtypeStruct(query.shape, bf),...  2.04 us

profile of v4, /device:TPU:79, one launch (start us, length us, event | category | flops | bytes accessed | tf_op | source)
XLA Modules:
  0.0 56.7 jit_solution(15843233348977178820)
XLA Ops:
  0.6 54.0 %shard_map.85 = (bf16[4,2,128,256]{3,2,1,0:T(8,128)(2,1)}, bf16[4,2,128,128]{3,2,1,0:T(8,128)(2,1)}) custom-call(bf16[128,2048]{1,0:T(8,128)(2,1)} %bitcast.5, bf16[128,512]{1,0:T(8,128)(2,1)} %bitcast.8, bf16[128,512]{1,0:T(8,128)(2,1)} %bitcast.9, bf16[128,2048]{1,0:T(8,128)(2,1)} %bitcast.6, bf16[128,2048]{1,0:T(8,128)(2,1)} %bitcast.7, s32[1,128]{1,0:T(1,128)} %id_ref.1), custom_call_target="tpu_custom_call" | custom-call | tf_op jit(solution)/shard_map/pallas_call | solution.py:528
  54.6 2.0 %shard_map.86 = (bf16[1,128,2048]{2,1,0:T(8,128)(2,1)}, bf16[1,128,512]{2,1,0:T(8,128)(2,1)}, bf16[1,128,512]{2,1,0:T(8,128)(2,1)}) custom-call(bf16[4,2,128,256]{3,2,1,0:T(8,128)(2,1)} %get-tuple-element.5.dq_raw, bf16[4,2,128,128]{3,2,1,0:T(8,128)(2,1)} %get-tuple-element.6.kv_raw), custom_call_target="tpu_custom_call" | custom-call | tf_op jit(solution)/shard_map/pallas_call | solution.py:576

commit v5 on v4

--- a/solution.py
+++ b/solution.py
@@ -24,15 +24,15 @@
 
 def kernel(
     rows, back,
-    q_ref, k_ref, v_ref, do_ref, o_ref, id_ref,
+    q_hbm, k_ref, v_ref, do_hbm, o_hbm, id_ref,
     dqrecv, frecv,
-    ksend, kbuf, vbuf, k_x, k_t,
+    q_ref, do_ref, o_ref, ksend, kbuf, vbuf, k_x, k_t,
     rdsend, qbuf, dobuf, rdbuf, q_x, q_h, do_t, do_h, rd_h,
     e_all, m_all, top_all, inv_all, p_low, s_low, dq_t,
     kv_acc, xrecv, ysend, yrecv, fsend, dqsend,
     ks, kr, vs, vr, qs, qr, gs, gr, rs, rr,
     kps, kpr, vps, vpr, kys, kyr, vys, vyr,
-    xs, xr, ys, yr, fs, fr, ds, dr,
+    xs, xr, ys, yr, fs, fr, ds, dr, ins,
 ):
     tok = q_ref.shape[0]
     span = 2 * tok
@@ -54,6 +54,12 @@
 
     partner = at(y, x, other)
 
+    q_in = pltpu.make_async_copy(q_hbm, q_ref, ins.at[0])
+    do_in = pltpu.make_async_copy(do_hbm, do_ref, ins.at[1])
+    o_in = pltpu.make_async_copy(o_hbm, o_ref, ins.at[2])
+    q_in.start()
+    do_in.start()
+    o_in.start()
     barrier = pltpu.get_barrier_semaphore()
     pl.semaphore_signal(barrier, inc=1, device_id=partner)
     for col in (mate, near, far):
@@ -84,8 +90,6 @@
         ksend[col, tok:, :] = barred
     kbuf[core, x] = ksend[x]
     vbuf[core, x] = v_ref[:, feats(x, 1)]
-    qbuf[x, core] = q_ref[:, pair_cols(x, core)]
-    dobuf[x, core] = do_ref[:, pair_cols(x, core)]
 
     pl.semaphore_wait(barrier, 2 * CHIPS - 1 + depth + reach)
 
@@ -173,6 +177,9 @@
 
         lax.fori_loop(0, CHIPS, one, 0)
 
+    q_in.wait()
+    q_copy(x, other).start()
+    q_copy(mate, core).start()
     for col in (mate, near, far):
         k_from(col).wait_recv()
     k_pass(0, core).start()
@@ -181,10 +188,14 @@
         v_from(col).wait_recv()
     v_pass(0, core).start()
     lax.fori_loop(1, reach + 1, start_v_row, 0)
-    q_copy(x, other).start()
-    for col in (mate, near, far):
+    for col in (near, far):
         for side in range(2):
             q_copy(col, side).start()
+    q_copy(mate, other).start()
+    qbuf[x, core] = q_ref[:, pair_cols(x, core)]
+    do_in.wait()
+    o_in.wait()
+    dobuf[x, core] = do_ref[:, pair_cols(x, core)]
 
     for col in range(CHIPS):
         for side in range(2):
@@ -225,8 +236,9 @@
         v_pass(r, other).wait_recv()
         return c
 
-    lax.fori_loop(1, depth + 1, pass_k_row, 0)
-    lax.fori_loop(1, depth + 1, have_k_row, 0)
+    @pl.when(depth > 0)
+    def _():
+        pass_k_row(1, 0)
 
     tiles = [(c, g, slice((c * PAIR + g) * span, (c * PAIR + g + 1) * span))
              for c in range(2) for g in range(PAIR)]
@@ -265,12 +277,37 @@
         top = 2 * y + a
         return a, top, jnp.minimum(top + 1, steps)
 
+    def powers(a, top, t, stats, causal):
+        place = place_of(top - t)
+        keys_x = k_x[pl.ds(2 * place, 2)].reshape(2 * span, 2 * hw)
+        out = []
+        for (c, g, cols), (m_run, l_run) in zip(tiles, stats):
+            s = nn(keys_x, q_x[a, :, cols])
+            if causal:
+                key_pos = lax.broadcasted_iota(jnp.int32, (2 * span, span), 0)
+                query_pos = lax.broadcasted_iota(jnp.int32, (2 * span, span), 1)
+                s = jnp.where(key_pos <= query_pos + c * span, s, MASKED_LOW)
+            m = jnp.max(s, axis=0, keepdims=True)
+            e = jnp.exp2((s - m) * LOG2_SCALE)
+            e_all[a, t, :, cols] = e
+            m_all[a, t, :, cols] = m
+            l = jnp.sum(e, axis=0, keepdims=True)
+            m_new = jnp.maximum(m_run, m)
+            l_run = (l_run * jnp.exp2((m_run - m_new) * LOG2_SCALE)
+                     + l * jnp.exp2((m - m_new) * LOG2_SCALE))
+            out.append((m_new, l_run))
+        return tuple(out)
+
+    def keep(a, stats):
+        top_all[a] = jnp.concatenate([m for m, _ in stats], axis=1)
+        inv_all[a] = jnp.concatenate([l for _, l in stats], axis=1)
+
+    def more_powers(a, top, start, stop):
+        stats = tuple((top_all[a, :, cols], inv_all[a, :, cols]) for _, _, cols in tiles)
+        keep(a, lax.fori_loop(start, stop, lambda t, now: powers(a, top, t, now, False), stats))
+
     def first_pass(p, carry):
         a, top, count = chunks_of(p)
-
-        @pl.when(p == 1)
-        def _():
-            lax.fori_loop(1, depth + 1, pass_v_row, 0)
 
         for c in range(2):
             qc = 2 * a + c
@@ -296,39 +333,37 @@
                 bars.astype(jnp.float32) == 0.0, 1.0, 0.0).astype(jnp.bfloat16)
         q_x[a, hw + DOC_ROWS:, :] = jnp.zeros((hw - DOC_ROWS, 2 * PAIR * span), jnp.bfloat16)
 
-        def powers(t, stats, causal):
-            place = place_of(top - t)
-            keys_x = k_x[pl.ds(2 * place, 2)].reshape(2 * span, 2 * hw)
-            out = []
-            for (c, g, cols), (m_run, l_run) in zip(tiles, stats):
-                s = nn(keys_x, q_x[a, :, cols])
-                if causal:
-                    key_pos = lax.broadcasted_iota(jnp.int32, (2 * span, span), 0)
-                    query_pos = lax.broadcasted_iota(jnp.int32, (2 * span, span), 1)
-                    s = jnp.where(key_pos <= query_pos + c * span, s, MASKED_LOW)
-                m = jnp.max(s, axis=0, keepdims=True)
-                e = jnp.exp2((s - m) * LOG2_SCALE)
-                e_all[a, t, :, cols] = e
-                m_all[a, t, :, cols] = m
-                l = jnp.sum(e, axis=0, keepdims=True)
-                m_new = jnp.maximum(m_run, m)
-                l_run = (l_run * jnp.exp2((m_run - m_new) * LOG2_SCALE)
-                         + l * jnp.exp2((m - m_new) * LOG2_SCALE))
-                out.append((m_new, l_run))
-            return tuple(out)
-
-        def later_powers(t, stats):
-            return powers(t, stats, False)
-
         start = tuple((jnp.full((1, span), MASKED_LOW, jnp.float32),
                        jnp.zeros((1, span), jnp.float32)) for _ in tiles)
-        stats = powers(0, start, True)
-        stats = lax.fori_loop(1, count, later_powers, stats)
-        top_all[a] = jnp.concatenate([m for m, _ in stats], axis=1)
-        inv_all[a] = 1.0 / jnp.concatenate([l for _, l in stats], axis=1)
+        keep(a, powers(a, top, 0, start, True))
+
+        @pl.when((p == 0) & (depth > 0))
+        def _():
+            have_k_row(1, 0)
+
+        @pl.when((p == 1) & (depth > 1))
+        def _():
+            lax.fori_loop(2, depth + 1, pass_k_row, 0)
+
+        more_powers(a, top, 1, jnp.minimum(count, 3 + a))
         return carry
 
+    def farthest_row(p, carry):
+        a, top, count = chunks_of(p)
+        more_powers(a, top, 3 + a, count)
+        return carry
+
     lax.fori_loop(0, 2, first_pass, 0)
+
+    @pl.when(depth > 1)
+    def _():
+        lax.fori_loop(2, depth + 1, have_k_row, 0)
+        pass_v_row(1, 0)
+        lax.fori_loop(0, 2, farthest_row, 0)
+
+    for a in range(2):
+        inv_all[a] = 1.0 / inv_all[a]
+
     def take_gradients(p, carry):
         a = (x // 2 + p) % 2
         for c in range(2):
@@ -348,27 +383,34 @@
                 [rdbuf[qc, 0, g:g + 1, :], rdbuf[qc, 1, g:g + 1, :]], axis=1)
         return carry
 
-    lax.fori_loop(0, 2, take_gradients, 0)
-    lax.fori_loop(0, depth + 1, have_v_row, 0)
+    @pl.when(depth == 1)
+    def _():
+        pass_v_row(1, 0)
+
+    take_gradients(0, 0)
+    have_v_row(0, 0)
+
+    @pl.when(depth > 0)
+    def _():
+        have_v_row(1, 0)
 
     own = x // 2
     away = 1 - own
     low = 2 * y - 2 * back
-    lead = 1 + away
-    shared = 4 * back - 1
+    ahead = 2 * back - 1
+    late = 2 * ahead + 1
 
     def item(n):
-        i = n - lead
-        j = i - 1
-        in_lead, in_tail = n < lead, i >= shared
+        in_own, in_low, in_far = n < ahead, n == ahead, n < late
+        in_lead = n < late + 1 + away
         block = jnp.where(
-            in_lead, 2 * y + n,
-            jnp.where(in_tail, 2 * y + i - shared,
-                      jnp.where(i == 0, low, low + 1 + j // 2)))
+            in_own, jnp.where(n < 2, 2 * y - 2 + n, low - 1 + n),
+            jnp.where(in_far, low + n - ahead,
+                      jnp.where(in_lead, 2 * y + n - late, 2 * y + n - late - 1 - away)))
         a = jnp.where(
-            in_lead, away,
-            jnp.where(in_tail, own, jnp.where(i == 0, 0, jnp.where(j % 2 == 0, away, own))))
-        final = jnp.where(in_lead, n == 1, in_tail | (i % 2 == 0))
+            in_own, own,
+            jnp.where(in_low, 0, jnp.where(in_lead, away, own)))
+        final = jnp.where(in_own, False, jnp.where(in_far, True, ~in_lead | (n == late + 1)))
         return a, block, final & (block >= 0)
 
     def send_queries(a):
@@ -387,6 +429,18 @@
 
     def terms(n, c):
         a, block, final = item(n)
+
+        @pl.when((n == 1) & (depth > 1))
+        def _():
+            lax.fori_loop(2, depth + 1, pass_v_row, 0)
+
+        @pl.when((n == 2) & (depth > 1))
+        def _():
+            lax.fori_loop(2, depth + 1, have_v_row, 0)
+
+        @pl.when(n == ahead)
+        def _():
+            take_gradients(1, 0)
 
         @pl.when(block >= 0)
         def _():
@@ -419,13 +473,13 @@
         def _():
             settle(before)
 
-        @pl.when(n == lead + shared - 2)
+        @pl.when(n == late + away)
         def _():
             send_queries(away)
 
         return c
 
-    last = lead + shared + own
+    last = late + 2
     lax.fori_loop(0, last + 1, terms, 0)
     send_queries(own)
     settle(item(last)[1])
@@ -524,6 +578,7 @@
     far = max(back, 1)
     bf, f32 = jnp.bfloat16, jnp.float32
     vmem = pl.BlockSpec(memory_space=pltpu.VMEM)
+    anywhere = pl.BlockSpec(memory_space=pl.ANY)
     dma = pltpu.SemaphoreType.DMA
     dq_raw, kv_raw = pl.pallas_call(
         functools.partial(kernel, rows, back),
@@ -531,9 +586,12 @@
             jax.ShapeDtypeStruct((CHIPS, 2, tok, width), bf),
             jax.ShapeDtypeStruct((CHIPS, 2, tok, hw), bf),
         ),
-        in_specs=[vmem] * 6,
+        in_specs=[anywhere, vmem, vmem, anywhere, anywhere, vmem],
         out_specs=(vmem,) * 2,
         scratch_shapes=[
+            pltpu.VMEM((tok, query.shape[2]), bf),
+            pltpu.VMEM((tok, query.shape[2]), bf),
+            pltpu.VMEM((tok, query.shape[2]), bf),
             pltpu.VMEM((CHIPS, tok + DOC_ROWS, hw), bf),
             pltpu.VMEM((2, slots, tok + DOC_ROWS, hw), bf),
             pltpu.VMEM((2, slots, tok, hw), bf),
@@ -568,6 +626,7 @@
             dma((back + 1,)), dma((back + 1,)), dma((back + 1,)), dma((back + 1,)),
             dma((slots // 2,)), dma((slots // 2,)), dma((far, 2)), dma((far, 2)),
             dma((CHIPS,)), dma((CHIPS,)), dma((CHIPS, 2)), dma((CHIPS, 2)),
+            dma((3,)),
         ],
         compiler_params=pltpu.CompilerParams(
             collective_id=0, has_side_effects=True, vmem_limit_bytes=56 * 1024 * 1024,

time: 56.8 us -> 54.1 us (0.952)
  Pallas kernels: 56 us -> 53 us
    pallas_call x1, Pallas kernels: 54 us -> 51 us  [on_device(): pl.pallas_call(functools.partial(kernel, rows, back), out_shape=(jax.Shap...]
where the time goes in v5:
time: 54.1 us; the launch traced here: 53.7 us
  Pallas kernels  53 us (98%)
  between operations  0.64 us (1%)
    pallas_call x1, Pallas kernels, on_device(): pl.pallas_call(functools.partial(kernel, rows, back), out_shape=(jax.Shap...  51 us
    pallas_call x1, Pallas kernels, on_device(): pl.pallas_call(lay_out, out_shape=(jax.ShapeDtypeStruct(query.shape, bf),...  2.04 us

profile of v5, /device:TPU:79, one launch (start us, length us, event | category | flops | bytes accessed | tf_op | source)
XLA Modules:
  0.0 53.7 jit_solution(3458594362828791573)
XLA Ops:
  0.6 51.0 %shard_map.85 = (bf16[4,2,128,256]{3,2,1,0:T(8,128)(2,1)}, bf16[4,2,128,128]{3,2,1,0:T(8,128)(2,1)}) custom-call(bf16[128,2048]{1,0:T(8,128)(2,1)} %bitcast.5, bf16[128,512]{1,0:T(8,128)(2,1)} %bitcast.8, bf16[128,512]{1,0:T(8,128)(2,1)} %bitcast.9, bf16[128,2048]{1,0:T(8,128)(2,1)} %bitcast.6, bf16[128,2048]{1,0:T(8,128)(2,1)} %bitcast.7, s32[1,128]{1,0:T(1,128)} %id_ref.1), custom_call_target="tpu_custom_call" | custom-call | tf_op jit(solution)/shard_map/pallas_call | solution.py:583
  51.6 2.0 %shard_map.86 = (bf16[1,128,2048]{2,1,0:T(8,128)(2,1)}, bf16[1,128,512]{2,1,0:T(8,128)(2,1)}, bf16[1,128,512]{2,1,0:T(8,128)(2,1)}) custom-call(bf16[4,2,128,256]{3,2,1,0:T(8,128)(2,1)} %get-tuple-element.5.dq_raw, bf16[4,2,128,128]{3,2,1,0:T(8,128)(2,1)} %get-tuple-element.6.kv_raw), custom_call_target="tpu_custom_call" | custom-call | tf_op jit(solution)/shard_map/pallas_call | solution.py:635

commit v6 on v5

--- a/solution.py
+++ b/solution.py
@@ -184,14 +184,14 @@
         k_from(col).wait_recv()
     k_pass(0, core).start()
     lax.fori_loop(1, reach + 1, start_k_row, 0)
+    q_copy(mate, other).start()
+    for col in (near, far):
+        for side in range(2):
+            q_copy(col, side).start()
     for col in (mate, near, far):
         v_from(col).wait_recv()
     v_pass(0, core).start()
     lax.fori_loop(1, reach + 1, start_v_row, 0)
-    for col in (near, far):
-        for side in range(2):
-            q_copy(col, side).start()
-    q_copy(mate, other).start()
     qbuf[x, core] = q_ref[:, pair_cols(x, core)]
     do_in.wait()
     o_in.wait()
@@ -277,19 +277,27 @@
         top = 2 * y + a
         return a, top, jnp.minimum(top + 1, steps)
 
-    def powers(a, top, t, stats, causal):
+    FIRST, BETWEEN, LAST = 0, 1, 2
+
+    def key_rows(kind, c):
+        low = 1 if kind == LAST and c == 1 else 0
+        high = 1 if kind == FIRST and c == 0 else 2
+        return low * span, high * span
+
+    def powers(a, top, t, stats, kind):
         place = place_of(top - t)
         keys_x = k_x[pl.ds(2 * place, 2)].reshape(2 * span, 2 * hw)
         out = []
         for (c, g, cols), (m_run, l_run) in zip(tiles, stats):
-            s = nn(keys_x, q_x[a, :, cols])
-            if causal:
-                key_pos = lax.broadcasted_iota(jnp.int32, (2 * span, span), 0)
-                query_pos = lax.broadcasted_iota(jnp.int32, (2 * span, span), 1)
+            low, high = key_rows(kind, c)
+            s = nn(keys_x[low:high], q_x[a, :, cols])
+            if kind == FIRST:
+                key_pos = lax.broadcasted_iota(jnp.int32, (high - low, span), 0)
+                query_pos = lax.broadcasted_iota(jnp.int32, (high - low, span), 1)
                 s = jnp.where(key_pos <= query_pos + c * span, s, MASKED_LOW)
             m = jnp.max(s, axis=0, keepdims=True)
             e = jnp.exp2((s - m) * LOG2_SCALE)
-            e_all[a, t, :, cols] = e
+            e_all[a, t, low:high, cols] = e
             m_all[a, t, :, cols] = m
             l = jnp.sum(e, axis=0, keepdims=True)
             m_new = jnp.maximum(m_run, m)
@@ -304,7 +312,7 @@
 
     def more_powers(a, top, start, stop):
         stats = tuple((top_all[a, :, cols], inv_all[a, :, cols]) for _, _, cols in tiles)
-        keep(a, lax.fori_loop(start, stop, lambda t, now: powers(a, top, t, now, False), stats))
+        keep(a, lax.fori_loop(start, stop, lambda t, now: powers(a, top, t, now, BETWEEN), stats))
 
     def first_pass(p, carry):
         a, top, count = chunks_of(p)
@@ -335,7 +343,7 @@
 
         start = tuple((jnp.full((1, span), MASKED_LOW, jnp.float32),
                        jnp.zeros((1, span), jnp.float32)) for _ in tiles)
-        keep(a, powers(a, top, 0, start, True))
+        keep(a, powers(a, top, 0, start, FIRST))
 
         @pl.when((p == 0) & (depth > 0))
         def _():
@@ -350,7 +358,9 @@
 
     def farthest_row(p, carry):
         a, top, count = chunks_of(p)
-        more_powers(a, top, 3 + a, count)
+        more_powers(a, top, 3 + a, steps - 1)
+        stats = tuple((top_all[a, :, cols], inv_all[a, :, cols]) for _, _, cols in tiles)
+        keep(a, powers(a, top, steps - 1, stats, LAST))
         return carry
 
     lax.fori_loop(0, 2, first_pass, 0)
@@ -388,29 +398,29 @@
         pass_v_row(1, 0)
 
     take_gradients(0, 0)
-    have_v_row(0, 0)
-
-    @pl.when(depth > 0)
-    def _():
-        have_v_row(1, 0)
+    lax.fori_loop(2, depth + 1, pass_v_row, 0)
+    take_gradients(1, 0)
+    lax.fori_loop(0, depth + 1, have_v_row, 0)
 
     own = x // 2
     away = 1 - own
     low = 2 * y - 2 * back
-    ahead = 2 * back - 1
-    late = 2 * ahead + 1
+    middle = 4 + away
+    tail = middle + 4
 
     def item(n):
-        in_own, in_low, in_far = n < ahead, n == ahead, n < late
-        in_lead = n < late + 1 + away
+        in_low, in_lead, in_middle = n < 3, n < middle, n < tail
+        k = n - middle
         block = jnp.where(
-            in_own, jnp.where(n < 2, 2 * y - 2 + n, low - 1 + n),
-            jnp.where(in_far, low + n - ahead,
-                      jnp.where(in_lead, 2 * y + n - late, 2 * y + n - late - 1 - away)))
+            in_low, low + (n + 1) // 2,
+            jnp.where(in_lead, 2 * y + n - 3,
+                      jnp.where(in_middle, 2 * y - 2 + k // 2, 2 * y + n - tail)))
         a = jnp.where(
-            in_own, own,
-            jnp.where(in_low, 0, jnp.where(in_lead, away, own)))
-        final = jnp.where(in_own, False, jnp.where(in_far, True, ~in_lead | (n == late + 1)))
+            in_low, jnp.where(n == 0, 0, jnp.where(n == 1, away, own)),
+            jnp.where(in_lead, away,
+                      jnp.where(in_middle, jnp.where(k % 2 == 0, away, own), own)))
+        final = jnp.where(
+            in_low, n != 1, jnp.where(in_lead, n == 4, ~in_middle | (k % 2 == 1)))
         return a, block, final & (block >= 0)
 
     def send_queries(a):
@@ -427,41 +437,57 @@
                 def _():
                     dq_copy(qc, side).start()
 
+    def add_terms(a, t, block, kind):
+        place = place_of(block)
+        v_both = jnp.concatenate(
+            [vbuf[i, 2 * place + u] for u in range(2) for i in range(2)], axis=0)
+        ratio = jnp.exp2((m_all[a, t] - top_all[a]) * LOG2_SCALE) * inv_all[a]
+        for c, _, cols in tiles:
+            low, high = key_rows(kind, c)
+            dp = nn(v_both[low:high], do_t[a, :, cols])
+            pr = e_all[a, t, low:high, cols] * ratio[:, cols]
+            p_low[low:high, cols] = pr.astype(jnp.bfloat16)
+            s_low[low:high, cols] = (pr * (dp - rd_h[a, :, cols])).astype(jnp.bfloat16)
+
+        def add_keys(low, high, cols):
+            dv = nn(p_low[low:high, cols], do_h[a, cols, :])
+            dk = nn(s_low[low:high, cols], q_h[a, cols, :]) * SCALE
+            for start in range(low, high, tok):
+                u, side = start // span, start // tok % 2
+                piece = slice(start - low, start - low + tok)
+                kv_acc[place, side, u, 0] += dk[piece]
+                kv_acc[place, side, u, 1] += dv[piece]
+
+        every = 2 * PAIR * span
+        k_both = jnp.concatenate([k_t[2 * place], k_t[2 * place + 1]], axis=1)
+        if kind == BETWEEN:
+            add_keys(0, 2 * span, slice(0, every))
+            dq_t[a] += nn(k_both, s_low[...])
+        else:
+            cut = slice(every // 2, every) if kind == FIRST else slice(0, every // 2)
+            add_keys(0, span, slice(0, every) if kind == FIRST else cut)
+            add_keys(span, 2 * span, slice(0, every) if kind == LAST else cut)
+            for c in range(2):
+                low, high = key_rows(kind, c)
+                cols = slice(c * every // 2, (c + 1) * every // 2)
+                dq_t[a, :, cols] += nn(k_both[:, low:high], s_low[low:high, cols])
+
     def terms(n, c):
         a, block, final = item(n)
 
-        @pl.when((n == 1) & (depth > 1))
-        def _():
-            lax.fori_loop(2, depth + 1, pass_v_row, 0)
-
-        @pl.when((n == 2) & (depth > 1))
-        def _():
-            lax.fori_loop(2, depth + 1, have_v_row, 0)
-
-        @pl.when(n == ahead)
-        def _():
-            take_gradients(1, 0)
-
-        @pl.when(block >= 0)
-        def _():
-            t = 2 * y + a - block
-            place = place_of(block)
-            v_both = jnp.concatenate(
-                [vbuf[i, 2 * place + u] for u in range(2) for i in range(2)], axis=0)
-            ratio = jnp.exp2((m_all[a, t] - top_all[a]) * LOG2_SCALE) * inv_all[a]
-            for _, _, cols in tiles:
-                dp = nn(v_both, do_t[a, :, cols])
-                pr = e_all[a, t, :, cols] * ratio[:, cols]
-                p_low[:, cols] = pr.astype(jnp.bfloat16)
-                s_low[:, cols] = (pr * (dp - rd_h[a, :, cols])).astype(jnp.bfloat16)
-            dv = nn(p_low[...], do_h[a])
-            dk = nn(s_low[...], q_h[a]) * SCALE
-            for u in range(2):
-                for side in range(2):
-                    piece = slice((2 * u + side) * tok, (2 * u + side + 1) * tok)
-                    kv_acc[place, side, u, 0] += dk[piece]
-                    kv_acc[place, side, u, 1] += dv[piece]
-            dq_t[a] += nn(jnp.concatenate([k_t[2 * place], k_t[2 * place + 1]], axis=1), s_low[...])
+        t = 2 * y + a - block
+
+        @pl.when((block >= 0) & (t == 0))
+        def _():
+            add_terms(a, t, block, FIRST)
+
+        @pl.when((block >= 0) & (t > 0) & (t < steps - 1))
+        def _():
+            add_terms(a, t, block, BETWEEN)
+
+        @pl.when((block >= 0) & (t == steps - 1))
+        def _():
+            add_terms(a, t, block, LAST)
 
         @pl.when(final)
         def _():
@@ -473,13 +499,13 @@
         def _():
             settle(before)
 
-        @pl.when(n == late + away)
+        @pl.when(n == middle + 2)
         def _():
             send_queries(away)
 
         return c
 
-    last = late + 2
+    last = tail + own
     lax.fori_loop(0, last + 1, terms, 0)
     send_queries(own)
     settle(item(last)[1])

time: 54.1 us -> 53.4 us (0.987)
  Pallas kernels: 53 us -> 51.8 us
    pallas_call x1, Pallas kernels: 51 us -> 49.8 us  [on_device(): pl.pallas_call(functools.partial(kernel, rows, back), out_shape=(jax.Shap...]
where the time goes in v6:
time: 53.4 us; the launch traced here: 52.4 us
  Pallas kernels  51.8 us (97%)
  between operations  0.64 us (1%)
    pallas_call x1, Pallas kernels, on_device(): pl.pallas_call(functools.partial(kernel, rows, back), out_shape=(jax.Shap...  49.8 us
    pallas_call x1, Pallas kernels, on_device(): pl.pallas_call(lay_out, out_shape=(jax.ShapeDtypeStruct(query.shape, bf),...  2.04 us

profile of v6, /device:TPU:79, one launch (start us, length us, event | category | flops | bytes accessed | tf_op | source)
XLA Modules:
  0.0 52.4 jit_solution(8305991061625391936)
XLA Ops:
  0.6 49.8 %shard_map.85 = (bf16[4,2,128,256]{3,2,1,0:T(8,128)(2,1)}, bf16[4,2,128,128]{3,2,1,0:T(8,128)(2,1)}) custom-call(bf16[128,2048]{1,0:T(8,128)(2,1)} %bitcast.5, bf16[128,512]{1,0:T(8,128)(2,1)} %bitcast.8, bf16[128,512]{1,0:T(8,128)(2,1)} %bitcast.9, bf16[128,2048]{1,0:T(8,128)(2,1)} %bitcast.6, bf16[128,2048]{1,0:T(8,128)(2,1)} %bitcast.7, s32[1,128]{1,0:T(1,128)} %id_ref.1), custom_call_target="tpu_custom_call" | custom-call | tf_op jit(solution)/shard_map/pallas_call | solution.py:609
  50.4 2.0 %shard_map.86 = (bf16[1,128,2048]{2,1,0:T(8,128)(2,1)}, bf16[1,128,512]{2,1,0:T(8,128)(2,1)}, bf16[1,128,512]{2,1,0:T(8,128)(2,1)}) custom-call(bf16[4,2,128,256]{3,2,1,0:T(8,128)(2,1)} %get-tuple-element.5.dq_raw, bf16[4,2,128,128]{3,2,1,0:T(8,128)(2,1)} %get-tuple-element.6.kv_raw), custom_call_target="tpu_custom_call" | custom-call | tf_op jit(solution)/shard_map/pallas_call | solution.py:661

commit v7 on v6

--- a/solution.py
+++ b/solution.py
@@ -165,17 +165,17 @@
         return c
 
     def build_keys(r):
-        def one(i, c):
+        bars = [jnp.concatenate([kbuf[side, r * CHIPS + i, tok:, :] for side in range(2)], axis=1)
+                for i in range(CHIPS)]
+        pad = jnp.zeros((hw - CHIPS * DOC_ROWS, span), jnp.bfloat16)
+        turned = jnp.transpose(jnp.concatenate(bars + [pad], axis=0)).astype(jnp.float32)
+        owner = lax.broadcasted_iota(jnp.int32, (span, hw), 1) // DOC_ROWS
+        for i in range(CHIPS):
             slot = r * CHIPS + i
             both = jnp.concatenate([kbuf[0, slot, :tok, :], kbuf[1, slot, :tok, :]], axis=0)
-            bars = jnp.concatenate([kbuf[0, slot, tok:, :], kbuf[1, slot, tok:, :]], axis=1)
-            pad = jnp.zeros((hw - DOC_ROWS, span), jnp.bfloat16)
             k_x[slot, :, :hw] = both
-            k_x[slot, :, hw:] = jnp.transpose(jnp.concatenate([bars, pad], axis=0))
+            k_x[slot, :, hw:] = jnp.where(owner == i, turned, 0.0).astype(jnp.bfloat16)
             k_t[slot] = jnp.transpose(both)
-            return c
-
-        lax.fori_loop(0, CHIPS, one, 0)
 
     q_in.wait()
     q_copy(x, other).start()
@@ -337,9 +337,11 @@
             q_h[a, cols, :] = both
             q_x[a, :hw, cols] = jnp.transpose(both)
             bars = jnp.concatenate([kbuf[0, qc, tok:, :], kbuf[1, qc, tok:, :]], axis=1)
-            q_x[a, hw:hw + DOC_ROWS, cols] = jnp.where(
-                bars.astype(jnp.float32) == 0.0, 1.0, 0.0).astype(jnp.bfloat16)
-        q_x[a, hw + DOC_ROWS:, :] = jnp.zeros((hw - DOC_ROWS, 2 * PAIR * span), jnp.bfloat16)
+            match = jnp.where(bars.astype(jnp.float32) == 0.0, 1.0, 0.0).astype(jnp.bfloat16)
+            for i in range(CHIPS):
+                q_x[a, hw + i * DOC_ROWS:hw + (i + 1) * DOC_ROWS, cols] = match
+        q_x[a, hw + CHIPS * DOC_ROWS:, :] = jnp.zeros(
+            (hw - CHIPS * DOC_ROWS, 2 * PAIR * span), jnp.bfloat16)
 
         start = tuple((jnp.full((1, span), MASKED_LOW, jnp.float32),
                        jnp.zeros((1, span), jnp.float32)) for _ in tiles)
@@ -398,35 +400,34 @@
         pass_v_row(1, 0)
 
     take_gradients(0, 0)
-    lax.fori_loop(2, depth + 1, pass_v_row, 0)
+    have_v_row(0, 0)
     take_gradients(1, 0)
-    lax.fori_loop(0, depth + 1, have_v_row, 0)
+
+    @pl.when(depth > 0)
+    def _():
+        have_v_row(1, 0)
 
     own = x // 2
     away = 1 - own
     low = 2 * y - 2 * back
-    middle = 4 + away
-    tail = middle + 4
+    close = 8 + away
 
     def item(n):
-        in_low, in_lead, in_middle = n < 3, n < middle, n < tail
-        k = n - middle
+        in_far, in_lead = (n >= 2) & (n < 5), n < close
         block = jnp.where(
-            in_low, low + (n + 1) // 2,
-            jnp.where(in_lead, 2 * y + n - 3,
-                      jnp.where(in_middle, 2 * y - 2 + k // 2, 2 * y + n - tail)))
-        a = jnp.where(
-            in_low, jnp.where(n == 0, 0, jnp.where(n == 1, away, own)),
-            jnp.where(in_lead, away,
-                      jnp.where(in_middle, jnp.where(k % 2 == 0, away, own), own)))
-        final = jnp.where(
-            in_low, n != 1, jnp.where(in_lead, n == 4, ~in_middle | (k % 2 == 1)))
+            n < 2, 2 * y - 2,
+            jnp.where(in_far, low + (n - 1) // 2,
+                      jnp.where(n < 7, 2 * y - 1,
+                                jnp.where(in_lead, 2 * y + n - 7, 2 * y + n - close))))
+        second = (n == 1) | (n == 4) | (n == 6)
+        a = jnp.where(n == 2, 0, jnp.where(second, own, jnp.where(in_lead, away, own)))
+        final = second | (n == 2) | (n == 8) | (n >= close)
         return a, block, final & (block >= 0)
 
     def send_queries(a):
         for c, g, cols in tiles:
             qc = 2 * a + c
-            piece = jnp.transpose(dq_t[a, :, cols] * SCALE).astype(jnp.bfloat16)
+            piece = jnp.transpose((dq_t[a, :, cols] * SCALE).astype(jnp.bfloat16))
             head = slice(g * hw, (g + 1) * hw)
             dqsend[qc, 0, :, head] = piece[:tok]
             dqsend[qc, 1, :, head] = piece[tok:]
@@ -477,6 +478,14 @@
 
         t = 2 * y + a - block
 
+        @pl.when((n == 0) & (depth > 1))
+        def _():
+            lax.fori_loop(2, depth + 1, pass_v_row, 0)
+
+        @pl.when((n == 2) & (depth > 1))
+        def _():
+            lax.fori_loop(2, depth + 1, have_v_row, 0)
+
         @pl.when((block >= 0) & (t == 0))
         def _():
             add_terms(a, t, block, FIRST)
@@ -499,13 +508,13 @@
         def _():
             settle(before)
 
-        @pl.when(n == middle + 2)
+        @pl.when(n == close - 1)
         def _():
             send_queries(away)
 
         return c
 
-    last = tail + own
+    last = close + own
     lax.fori_loop(0, last + 1, terms, 0)
     send_queries(own)
     settle(item(last)[1])

time: 53.4 us -> 52.5 us (0.983)
  the two profiles are of different devices: /device:TPU:79 before, /device:TPU:48 now
where the time goes in v7:
time: 52.5 us; the launch traced here: 52.3 us
  Pallas kernels  51.7 us (98%)
  between operations  0.64 us (1%)
    pallas_call x1, Pallas kernels, on_device(): pl.pallas_call(functools.partial(kernel, rows, back), out_shape=(jax.Shap...  49.7 us
    pallas_call x1, Pallas kernels, on_device(): pl.pallas_call(lay_out, out_shape=(jax.ShapeDtypeStruct(query.shape, bf),...  2.04 us

profile of v7, /device:TPU:48, one launch (start us, length us, event | category | flops | bytes accessed | tf_op | source)
XLA Modules:
  0.0 52.3 jit_solution(7409247968958865560)
XLA Ops:
  0.6 49.7 %shard_map.85 = (bf16[4,2,128,256]{3,2,1,0:T(8,128)(2,1)}, bf16[4,2,128,128]{3,2,1,0:T(8,128)(2,1)}) custom-call(bf16[128,2048]{1,0:T(8,128)(2,1)} %bitcast.5, bf16[128,512]{1,0:T(8,128)(2,1)} %bitcast.8, bf16[128,512]{1,0:T(8,128)(2,1)} %bitcast.9, bf16[128,2048]{1,0:T(8,128)(2,1)} %bitcast.6, bf16[128,2048]{1,0:T(8,128)(2,1)} %bitcast.7, s32[1,128]{1,0:T(1,128)} %id_ref.1), custom_call_target="tpu_custom_call" | custom-call | tf_op jit(solution)/shard_map/pallas_call | solution.py:618
  50.3 2.0 %shard_map.86 = (bf16[1,128,2048]{2,1,0:T(8,128)(2,1)}, bf16[1,128,512]{2,1,0:T(8,128)(2,1)}, bf16[1,128,512]{2,1,0:T(8,128)(2,1)}) custom-call(bf16[4,2,128,256]{3,2,1,0:T(8,128)(2,1)} %get-tuple-element.5.dq_raw, bf16[4,2,128,128]{3,2,1,0:T(8,128)(2,1)} %get-tuple-element.6.kv_raw), custom_call_target="tpu_custom_call" | custom-call | tf_op jit(solution)/shard_map/pallas_call | solution.py:670

commit v8 on v7

--- a/solution.py
+++ b/solution.py
@@ -156,7 +156,8 @@
         k_copy(col).start()
     for col in (mate, far, near):
         v_copy(col).start()
-    def start_k_row(r, c):
+    def start_k_row(i, c):
+        r = jnp.where(y == 0, reach + 1 - i, i)
         k_row(r, at(y + r, x, core)).start()
         return c
 

time: 52.5 us -> 52.2 us (level)
  the two profiles are of different devices: /device:TPU:48 before, /device:TPU:79 now
where the time goes in v8:
time: 52.2 us; the launch traced here: 52.1 us
  Pallas kernels  51.4 us (98%)
  between operations  0.64 us (1%)
    pallas_call x1, Pallas kernels, on_device(): pl.pallas_call(functools.partial(kernel, rows, back), out_shape=(jax.Shap...  49.4 us
    pallas_call x1, Pallas kernels, on_device(): pl.pallas_call(lay_out, out_shape=(jax.ShapeDtypeStruct(query.shape, bf),...  2.04 us

profile of v8, /device:TPU:79, one launch (start us, length us, event | category | flops | bytes accessed | tf_op | source)
XLA Modules:
  0.0 52.1 jit_solution(1203542317552412041)
XLA Ops:
  0.6 49.4 %shard_map.85 = (bf16[4,2,128,256]{3,2,1,0:T(8,128)(2,1)}, bf16[4,2,128,128]{3,2,1,0:T(8,128)(2,1)}) custom-call(bf16[128,2048]{1,0:T(8,128)(2,1)} %bitcast.5, bf16[128,512]{1,0:T(8,128)(2,1)} %bitcast.8, bf16[128,512]{1,0:T(8,128)(2,1)} %bitcast.9, bf16[128,2048]{1,0:T(8,128)(2,1)} %bitcast.6, bf16[128,2048]{1,0:T(8,128)(2,1)} %bitcast.7, s32[1,128]{1,0:T(1,128)} %id_ref.1), custom_call_target="tpu_custom_call" | custom-call | tf_op jit(solution)/shard_map/pallas_call | solution.py:619
  50.0 2.0 %shard_map.86 = (bf16[1,128,2048]{2,1,0:T(8,128)(2,1)}, bf16[1,128,512]{2,1,0:T(8,128)(2,1)}, bf16[1,128,512]{2,1,0:T(8,128)(2,1)}) custom-call(bf16[4,2,128,256]{3,2,1,0:T(8,128)(2,1)} %get-tuple-element.5.dq_raw, bf16[4,2,128,128]{3,2,1,0:T(8,128)(2,1)} %get-tuple-element.6.kv_raw), custom_call_target="tpu_custom_call" | custom-call | tf_op jit(solution)/shard_map/pallas_call | solution.py:671
